TPU v7x, 32 devices: a whole 2x2x4 slice. The times are simulated.
32 devices in a mesh: req: 8 (over y, x, core), ctx: 4 (over z).
Axes of the slice: x: 2, y: 2, z: 4, core: 2. Of those that a mesh axis runs over, the one named last changes fastest.
Arguments:
- queries: bfloat16 [128, 8192], P(('req', 'ctx')), parts along dimension 0, may hold values from -15 to 15
- new_keys: bfloat16 [128, 512], P(('req', 'ctx')), parts along dimension 0, may hold values from -9 to 9
- new_values: bfloat16 [128, 512], P(('req', 'ctx')), parts along dimension 0, may hold values from -6 to 6
- cache_keys: bfloat16 [65536, 512], P(('req', 'ctx')), parts along dimension 0, may hold values from -6 to 6
- cache_values: bfloat16 [65536, 512], P(('req', 'ctx')), parts along dimension 0, may hold values from -6 to 6
- cache_length: int32 [8], P('req'), parts along dimension 0, may hold values from 2048 to 8191
- page_table: int32 [512], P('req'), parts along dimension 0, may hold values from 0 to 63, each once
Outputs:
- attended: bfloat16 [128, 8192], P(('req', 'ctx')), parts along dimension 0
There are 8 independent parts, one for each index of `req`. A program takes and returns all parts, laid end to end along the dimension named above; each array names one. Nothing has to cross between parts.
Inputs may be any that keep to these rules, and one draw needn't show every extreme that they name: A permutation: logical page p lies in physical rows page_table[p] * 128 to page_table[p] * 128 + 127.
All inputs are finite; a program needn't handle non-finite values.
Results may differ from a plain program's by a relative error of at most 0.004.
Values may be sent and summed in bfloat16 or wider, within the bound.
A program may use at most 64 MiB of HBM per device.

v0:
```python
import jax
import jax.numpy as jnp
from jax import lax
from jax.sharding import PartitionSpec as P

KVH = 4
HD = 128
PAGE = 128


floor_score = -1e30


def from_behind(x, axis, by):
    devices = lax.axis_size(axis)
    return lax.ppermute(x, axis, [(i, (i + by) % devices) for i in range(devices)])


def attend(queries, query_pos, keys, values, key_pos, key_ok):
    rows = queries.shape[0]
    heads = queries.shape[1] // HD
    grouped = queries.reshape(rows, KVH, heads // KVH, HD)
    key_count = keys.shape[0]
    keys_grouped = keys.reshape(key_count, KVH, HD)
    values_grouped = values.reshape(key_count, KVH, HD)
    scores = jnp.einsum(
        "rkgd,nkd->rkgn", grouped, keys_grouped, preferred_element_type=jnp.float32
    ) * HD ** (-0.5)
    allowed = key_ok[None, :] & (key_pos[None, :] <= query_pos[:, None])
    allowed = allowed[:, None, None, :]
    scores = jnp.where(allowed, scores, floor_score)
    top = jnp.max(scores, axis=3)
    weights = jnp.where(allowed, jnp.exp(scores - top[..., None]), 0.0)
    total = jnp.sum(weights, axis=3)
    mixed = jnp.einsum(
        "rkgn,nkd->rkgd",
        weights.astype(jnp.bfloat16),
        values_grouped,
        preferred_element_type=jnp.float32,
    )
    return (mixed.reshape(rows, heads * HD), top.reshape(rows, heads), total.reshape(rows, heads))


def combine(first, second):
    mixed_first, top_first, total_first = first
    mixed_second, top_second, total_second = second
    rows, heads = top_first.shape
    top = jnp.maximum(top_first, top_second)
    factor_first = jnp.exp(top_first - top)
    factor_second = jnp.exp(top_second - top)
    mixed = (
        mixed_first.reshape(rows, heads, HD) * factor_first[..., None]
        + mixed_second.reshape(rows, heads, HD) * factor_second[..., None]
    )
    return (
        mixed.reshape(rows, heads * HD),
        top,
        factor_first * total_first + factor_second * total_second,
    )


def empty_state(rows, heads):
    return (
        jnp.zeros((rows, heads * HD), jnp.float32),
        jnp.full((rows, heads), floor_score, jnp.float32),
        jnp.zeros((rows, heads), jnp.float32),
    )


def settle(moved):
    return (moved[0], moved[1], moved[2], moved[3])


def local(queries, new_keys, new_values, cache_keys, cache_values, cache_length, page_table):
    count = lax.axis_size("ctx")
    device = lax.axis_index("ctx")
    rows = queries.shape[0]
    heads = queries.shape[1] // HD
    local_pages = cache_keys.shape[0] // PAGE
    length = cache_length[0]
    slots = device * local_pages + lax.iota(jnp.int32, local_pages)
    hits = (page_table[:, None] == slots[None, :]).astype(jnp.int32)
    logical = jnp.sum(hits * lax.iota(jnp.int32, page_table.shape[0])[:, None], axis=0)
    cache_pos = (logical[:, None] * PAGE + lax.iota(jnp.int32, PAGE)[None, :]).reshape(-1)
    cache_live = cache_pos < length
    own_pos = length + device * rows + lax.iota(jnp.int32, rows)

    def attend_cache(held, positions):
        return attend(held, positions, cache_keys, cache_values, cache_pos, cache_live)

    keys_piece = lax.all_gather(new_keys, "ctx", axis=0, tiled=True)
    values_piece = lax.all_gather(new_values, "ctx", axis=0, tiled=True)
    piece_rows = keys_piece.shape[0]
    key_pos = length + lax.iota(jnp.int32, piece_rows)
    span_state = combine(
        empty_state(rows, heads),
        attend(queries, own_pos, keys_piece, values_piece, key_pos, jnp.ones((piece_rows,), bool)),
    )

    def hop_one(step, carry):
        held = carry[0]
        source = (device - step) % count
        positions = length + source * rows + lax.iota(jnp.int32, rows)
        state = combine(carry[1:4], attend_cache(held, positions))
        return settle(from_behind((held,) + state, "ctx", 1))

    final = lax.fori_loop(0, count, hop_one, (queries,) + empty_state(rows, heads))
    cycle_state = final[1:4]
    mixed, top, total = combine(cycle_state, span_state)
    result = mixed.reshape(rows, heads, HD) / total[..., None]
    return result.reshape(rows, heads * HD).astype(jnp.bfloat16)


def solution(mesh):
    in_specs = (
        P(("req", "ctx"), None),
        P(("req", "ctx"), None),
        P(("req", "ctx"), None),
        P(("req", "ctx"), None),
        P(("req", "ctx"), None),
        P("req"),
        P("req"),
    )
    out_specs = P(("req", "ctx"), None)
    return jax.shard_map(local, mesh=mesh, in_specs=in_specs, out_specs=out_specs, check_vma=False)
```

profile of v0, /device:TPU:0, one launch (start us, length us, event | category | flops | bytes accessed | tf_op | source)
XLA Modules:
  0.0 100.8 jit_solution(797764317220166402)
XLA Ops:
  2.4 14.9 %all-gather = bf16[4,4,512]{2,1,0:T(4,128)(2,1)S(1)} all-gather(bf16[1,4,512]{2,1,0:T(4,128)(2,1)} %bitcast.139), channel_id=1, replica_groups=mesh['req'=8,'ctx'=4] {'ctx'}, dimensions={0}, use_global_device_ids=true | all-gather | bytes 20480 | tf_op jit(solution)/shard_map/all_gather | solution.py:91
  17.4 13.3 %all-gather.1 = bf16[4,4,512]{2,1,0:T(4,128)(2,1)S(1)} all-gather(bf16[1,4,512]{2,1,0:T(4,128)(2,1)} %bitcast.140), channel_id=1, replica_groups=mesh['req'=8,'ctx'=4] {'ctx'}, dimensions={0}, use_global_device_ids=true | all-gather | bytes 20480 | tf_op jit(solution)/shard_map/all_gather | solution.py:92
  31.6 4.1 %reshape.248 = bf16[2048,4,128]{2,1,0:T(4,128)(2,1)} reshape(bf16[2048,512]{1,0:T(8,128)(2,1)} %param.12) | data formatting | bytes 4194304 | tf_op jit(solution)/shard_map/while/body/eval_jaxpr/reshape | solution.py:24
  35.7 2.0 %reshape.249 = bf16[2048,4,128]{2,1,0:T(4,128)(2,1)} reshape(bf16[2048,512]{1,0:T(8,128)(2,1)S(1)} %copy-done) | data formatting | bytes 4194304 | tf_op jit(solution)/shard_map/while/body/eval_jaxpr/reshape | solution.py:25
  37.8 61.5 %while.24 = (s32[]{:T(128)}, bf16[4,8192]{1,0:T(4,128)(2,1)S(1)}, f32[4,8192]{1,0:T(4,128)S(1)}, f32[4,64]{1,0:T(4,128)S(1)}, f32[4,64]{1,0:T(4,128)S(1)}, /*ind...) while((s32[]{:T(128)}, bf16[4,8192]{1,0:T(4,128)(2,1)S(1)}, ...), condition=%wide.wide.region_4.5_spmd.clone.clone, body=%wide.wide.region_1.4_spmd.clone.clone.sunk | while | flops 273275904 | bytes 21383816 | solution.py:107
  39.4 2.5 %fusion.68 = (f32[4,4,16]{2,0,1:T(4,128)S(1)}, f32[4,4,16,2048]{3,2,0,1:T(8,128)S(1)}) fusion(bf16[4,4,16,128]{3,2,1,0:T(8,128)(2,1)S(1)} %bitcast.134, bf16[2048,4,128,1]{2,1,0,3:T(4,128)(2,1)} %bitcast.132, pred[4,2048]{1,0:T(4,128)(4,1)S(1)} %compare_and_fusion.3), kind=kOutput, calls=%fused_computation.73.clone.clone.1 | convolution fusion | flops 135790336 | bytes 4269056 | tf_op jit(solution)/shard_map/while/body/eval_jaxpr/rkgd,nkd->rkgn/dot_general | solution.py:26
  42.5 1.0 %copy-done.1 = bf16[2048,4,128]{2,1,0:T(4,128)(2,1)S(1)} copy-done((bf16[2048,4,128]{2,1,0:T(4,128)(2,1)S(1)}, bf16[2048,4,128]{2,1,0:T(4,128)(2,1)}, u32[]{:S(2)}) %copy-start.1) | copy-done | bytes 2097176 | tf_op jit(solution)/shard_map/while
  44.9 1.6 %collective-permute-start.1 = (f32[4,8192]{1,0:T(4,128)S(1)}, f32[4,8192]{1,0:T(4,128)S(1)}, u32[]{:S(2)}, u32[]{:S(2)}) collective-permute-start(f32[4,8192]{1,0:T(4,128)S(1)} %fusion.71), channel_id=1, source_target_pairs={{0,1},{1,2},{2,3},{3,0},{4,5},{5,6},{6,7},{7,4},{8,9},{9,10},{10,1... | collective-permute-start | bytes 393224 | tf_op jit(solution)/shard_map/while/body/eval_jaxpr/ppermute | solution.py:16
  46.6 2.9 %collective-permute-start.2 = (f32[4,64]{1,0:T(4,128)S(1)}, f32[4,64]{1,0:T(4,128)S(1)}, u32[]{:S(2)}, u32[]{:S(2)}) collective-permute-start(f32[4,64]{1,0:T(4,128)S(1)} %get-tuple-element.508), channel_id=1, source_target_pairs={{0,1},{1,2},{2,3},{3,0},{4,5},{5,6},{6,7},{7,4},{8,9},{9,10},{10,1... | collective-permute-start | bytes 3080 | tf_op jit(solution)/shard_map/while/body/eval_jaxpr/ppermute | solution.py:16
  49.9 2.7 %collective-permute-done.2 = f32[4,64]{1,0:T(4,128)S(1)} collective-permute-done((f32[4,64]{1,0:T(4,128)S(1)}, f32[4,64]{1,0:T(4,128)S(1)}, u32[]{:S(2)}, u32[]{:S(2)}) %collective-permute-start.2) | collective-permute-done | bytes 1056 | tf_op jit(solution)/shard_map/while/body/eval_jaxpr/ppermute | solution.py:16
  52.6 2.2 %collective-permute-done.3 = f32[4,64]{1,0:T(4,128)S(1)} collective-permute-done((f32[4,64]{1,0:T(4,128)S(1)}, f32[4,64]{1,0:T(4,128)S(1)}, u32[]{:S(2)}, u32[]{:S(2)}) %collective-permute-start.3) | collective-permute-done | bytes 1056 | tf_op jit(solution)/shard_map/while/body/eval_jaxpr/ppermute | solution.py:16
  56.5 2.5 %fusion.68 = (f32[4,4,16]{2,0,1:T(4,128)S(1)}, f32[4,4,16,2048]{3,2,0,1:T(8,128)S(1)}) fusion(bf16[4,4,16,128]{3,2,1,0:T(8,128)(2,1)S(1)} %bitcast.134, bf16[2048,4,128,1]{2,1,0,3:T(4,128)(2,1)} %bitcast.132, pred[4,2048]{1,0:T(4,128)(4,1)S(1)} %compare_and_fusion.3), kind=kOutput, calls=%fused_computation.73.clone.clone.1 | convolution fusion | flops 135790336 | bytes 4269056 | tf_op jit(solution)/shard_map/while/body/eval_jaxpr/rkgd,nkd->rkgn/dot_general | solution.py:26
  62.9 4.1 %collective-permute-start.3 = (f32[4,64]{1,0:T(4,128)S(1)}, f32[4,64]{1,0:T(4,128)S(1)}, u32[]{:S(2)}, u32[]{:S(2)}) collective-permute-start(f32[4,64]{1,0:T(4,128)S(1)} %get-tuple-element.509), channel_id=1, source_target_pairs={{0,1},{1,2},{2,3},{3,0},{4,5},{5,6},{6,7},{7,4},{8,9},{9,10},{10,1... | collective-permute-start | bytes 3080 | tf_op jit(solution)/shard_map/while/body/eval_jaxpr/ppermute | solution.py:16
  67.0 2.5 %collective-permute-done.2 = f32[4,64]{1,0:T(4,128)S(1)} collective-permute-done((f32[4,64]{1,0:T(4,128)S(1)}, f32[4,64]{1,0:T(4,128)S(1)}, u32[]{:S(2)}, u32[]{:S(2)}) %collective-permute-start.2) | collective-permute-done | bytes 1056 | tf_op jit(solution)/shard_map/while/body/eval_jaxpr/ppermute | solution.py:16
  71.2 2.5 %fusion.68 = (f32[4,4,16]{2,0,1:T(4,128)S(1)}, f32[4,4,16,2048]{3,2,0,1:T(8,128)S(1)}) fusion(bf16[4,4,16,128]{3,2,1,0:T(8,128)(2,1)S(1)} %bitcast.134, bf16[2048,4,128,1]{2,1,0,3:T(4,128)(2,1)} %bitcast.132, pred[4,2048]{1,0:T(4,128)(4,1)S(1)} %compare_and_fusion.3), kind=kOutput, calls=%fused_computation.73.clone.clone.1 | convolution fusion | flops 135790336 | bytes 4269056 | tf_op jit(solution)/shard_map/while/body/eval_jaxpr/rkgd,nkd->rkgn/dot_general | solution.py:26
  76.7 1.1 %collective-permute-start.1 = (f32[4,8192]{1,0:T(4,128)S(1)}, f32[4,8192]{1,0:T(4,128)S(1)}, u32[]{:S(2)}, u32[]{:S(2)}) collective-permute-start(f32[4,8192]{1,0:T(4,128)S(1)} %fusion.71), channel_id=1, source_target_pairs={{0,1},{1,2},{2,3},{3,0},{4,5},{5,6},{6,7},{7,4},{8,9},{9,10},{10,1... | collective-permute-start | bytes 393224 | tf_op jit(solution)/shard_map/while/body/eval_jaxpr/ppermute | solution.py:16
  78.5 3.2 %collective-permute-start.3 = (f32[4,64]{1,0:T(4,128)S(1)}, f32[4,64]{1,0:T(4,128)S(1)}, u32[]{:S(2)}, u32[]{:S(2)}) collective-permute-start(f32[4,64]{1,0:T(4,128)S(1)} %get-tuple-element.509), channel_id=1, source_target_pairs={{0,1},{1,2},{2,3},{3,0},{4,5},{5,6},{6,7},{7,4},{8,9},{9,10},{10,1... | collective-permute-start | bytes 3080 | tf_op jit(solution)/shard_map/while/body/eval_jaxpr/ppermute | solution.py:16
  81.7 2.5 %collective-permute-done.2 = f32[4,64]{1,0:T(4,128)S(1)} collective-permute-done((f32[4,64]{1,0:T(4,128)S(1)}, f32[4,64]{1,0:T(4,128)S(1)}, u32[]{:S(2)}, u32[]{:S(2)}) %collective-permute-start.2) | collective-permute-done | bytes 1056 | tf_op jit(solution)/shard_map/while/body/eval_jaxpr/ppermute | solution.py:16
  85.9 2.5 %fusion.68 = (f32[4,4,16]{2,0,1:T(4,128)S(1)}, f32[4,4,16,2048]{3,2,0,1:T(8,128)S(1)}) fusion(bf16[4,4,16,128]{3,2,1,0:T(8,128)(2,1)S(1)} %bitcast.134, bf16[2048,4,128,1]{2,1,0,3:T(4,128)(2,1)} %bitcast.132, pred[4,2048]{1,0:T(4,128)(4,1)S(1)} %compare_and_fusion.3), kind=kOutput, calls=%fused_computation.73.clone.clone.1 | convolution fusion | flops 135790336 | bytes 4269056 | tf_op jit(solution)/shard_map/while/body/eval_jaxpr/rkgd,nkd->rkgn/dot_general | solution.py:26
  91.4 1.1 %collective-permute-start.1 = (f32[4,8192]{1,0:T(4,128)S(1)}, f32[4,8192]{1,0:T(4,128)S(1)}, u32[]{:S(2)}, u32[]{:S(2)}) collective-permute-start(f32[4,8192]{1,0:T(4,128)S(1)} %fusion.71), channel_id=1, source_target_pairs={{0,1},{1,2},{2,3},{3,0},{4,5},{5,6},{6,7},{7,4},{8,9},{9,10},{10,1... | collective-permute-start | bytes 393224 | tf_op jit(solution)/shard_map/while/body/eval_jaxpr/ppermute | solution.py:16
  92.5 1.1 %collective-permute-start = (bf16[4,8192]{1,0:T(4,128)(2,1)S(1)}, bf16[4,8192]{1,0:T(4,128)(2,1)S(1)}, u32[]{:S(2)}, u32[]{:S(2)}) collective-permute-start(bf16[4,8192]{1,0:T(4,128)(2,1)S(1)} %copy.166), channel_id=1, source_target_pairs={{0,1},{1,2},{2,3},{3,0},{4,5},{5,6},{6,7},{7,4},{8,9},{9,10},{10,1... | collective-permute-start | bytes 196616 | tf_op jit(solution)/shard_map/while/body/eval_jaxpr/ppermute | solution.py:16
  93.9 2.5 %collective-permute-start.3 = (f32[4,64]{1,0:T(4,128)S(1)}, f32[4,64]{1,0:T(4,128)S(1)}, u32[]{:S(2)}, u32[]{:S(2)}) collective-permute-start(f32[4,64]{1,0:T(4,128)S(1)} %get-tuple-element.509), channel_id=1, source_target_pairs={{0,1},{1,2},{2,3},{3,0},{4,5},{5,6},{6,7},{7,4},{8,9},{9,10},{10,1... | collective-permute-start | bytes 3080 | tf_op jit(solution)/shard_map/while/body/eval_jaxpr/ppermute | solution.py:16
  96.4 2.6 %collective-permute-done.2 = f32[4,64]{1,0:T(4,128)S(1)} collective-permute-done((f32[4,64]{1,0:T(4,128)S(1)}, f32[4,64]{1,0:T(4,128)S(1)}, u32[]{:S(2)}, u32[]{:S(2)}) %collective-permute-start.2) | collective-permute-done | bytes 1056 | tf_op jit(solution)/shard_map/while/body/eval_jaxpr/ppermute | solution.py:16
  99.7 1.1 %fusion.28 = bf16[4,8192]{1,0:T(4,128)(2,1)} fusion(f32[1,4,64,128]{3,2,1,0:T(8,128)S(1)} %get-tuple-element.370, f32[1,4,64,128]{3,2,1,0:T(8,128)S(1)} %get-tuple-element.371, f32[1,4,64,128]{3,2,1,0:T(8,128)S(1)} %get-tuple-element.372, f32[1,4,64,128]{3,2,1,0:T(8,128)S(1)} %bitcast.135, f32[1,4,64,128]{3,2,1,0:T(8,128)S(1)} %get-tuple-element.373, ...), kind=kLoop, calls=%fused_computation.42 | loop fusion | flops 229376 | bytes 983040 | tf_op jit(solution)/shard_map/convert_element_type | solution.py:111
  (117 shorter events, 20.3 us)
Async XLA Ops:
  31.6 4.1 %copy-start = (bf16[2048,512]{1,0:T(8,128)(2,1)S(1)}, bf16[2048,512]{1,0:T(8,128)(2,1)}, u32[]{:S(2)}) copy-start(bf16[2048,512]{1,0:T(8,128)(2,1)} %param.13) | copy-start | bytes 6291460
  41.9 1.6 %copy-start.1 = (bf16[2048,4,128]{2,1,0:T(4,128)(2,1)S(1)}, bf16[2048,4,128]{2,1,0:T(4,128)(2,1)}, u32[]{:S(2)}) copy-start(bf16[2048,4,128]{2,1,0:T(4,128)(2,1)} %get-tuple-element.553) | copy-start | bytes 6291460 | tf_op jit(solution)/shard_map/while
  44.9 9.9 %collective-permute-start.1 = (f32[4,8192]{1,0:T(4,128)S(1)}, f32[4,8192]{1,0:T(4,128)S(1)}, u32[]{:S(2)}, u32[]{:S(2)}) collective-permute-start(f32[4,8192]{1,0:T(4,128)S(1)} %fusion.71), channel_id=1, source_target_pairs={{0,1},{1,2},{2,3},{3,0},{4,5},{5,6},{6,7},{7,4},{8,9},{9,10},{10,1... | collective-permute-start | bytes 393224 | tf_op jit(solution)/shard_map/while/body/eval_jaxpr/ppermute | solution.py:16
  46.6 8.3 %collective-permute-start = (bf16[4,8192]{1,0:T(4,128)(2,1)S(1)}, bf16[4,8192]{1,0:T(4,128)(2,1)S(1)}, u32[]{:S(2)}, u32[]{:S(2)}) collective-permute-start(bf16[4,8192]{1,0:T(4,128)(2,1)S(1)} %copy.166), channel_id=1, source_target_pairs={{0,1},{1,2},{2,3},{3,0},{4,5},{5,6},{6,7},{7,4},{8,9},{9,10},{10,1... | collective-permute-start | bytes 196616 | tf_op jit(solution)/shard_map/while/body/eval_jaxpr/ppermute | solution.py:16
  46.6 6.0 %collective-permute-start.2 = (f32[4,64]{1,0:T(4,128)S(1)}, f32[4,64]{1,0:T(4,128)S(1)}, u32[]{:S(2)}, u32[]{:S(2)}) collective-permute-start(f32[4,64]{1,0:T(4,128)S(1)} %get-tuple-element.508), channel_id=1, source_target_pairs={{0,1},{1,2},{2,3},{3,0},{4,5},{5,6},{6,7},{7,4},{8,9},{9,10},{10,1... | collective-permute-start | bytes 3080 | tf_op jit(solution)/shard_map/while/body/eval_jaxpr/ppermute | solution.py:16
  49.5 5.4 %collective-permute-start.3 = (f32[4,64]{1,0:T(4,128)S(1)}, f32[4,64]{1,0:T(4,128)S(1)}, u32[]{:S(2)}, u32[]{:S(2)}) collective-permute-start(f32[4,64]{1,0:T(4,128)S(1)} %get-tuple-element.509), channel_id=1, source_target_pairs={{0,1},{1,2},{2,3},{3,0},{4,5},{5,6},{6,7},{7,4},{8,9},{9,10},{10,1... | collective-permute-start | bytes 3080 | tf_op jit(solution)/shard_map/while/body/eval_jaxpr/ppermute | solution.py:16
  59.0 1.6 %copy-start.1 = (bf16[2048,4,128]{2,1,0:T(4,128)(2,1)S(1)}, bf16[2048,4,128]{2,1,0:T(4,128)(2,1)}, u32[]{:S(2)}) copy-start(bf16[2048,4,128]{2,1,0:T(4,128)(2,1)} %get-tuple-element.553) | copy-start | bytes 6291460 | tf_op jit(solution)/shard_map/while
  62.0 7.6 %collective-permute-start.1 = (f32[4,8192]{1,0:T(4,128)S(1)}, f32[4,8192]{1,0:T(4,128)S(1)}, u32[]{:S(2)}, u32[]{:S(2)}) collective-permute-start(f32[4,8192]{1,0:T(4,128)S(1)} %fusion.71), channel_id=1, source_target_pairs={{0,1},{1,2},{2,3},{3,0},{4,5},{5,6},{6,7},{7,4},{8,9},{9,10},{10,1... | collective-permute-start | bytes 393224 | tf_op jit(solution)/shard_map/while/body/eval_jaxpr/ppermute | solution.py:16
  62.1 7.5 %collective-permute-start = (bf16[4,8192]{1,0:T(4,128)(2,1)S(1)}, bf16[4,8192]{1,0:T(4,128)(2,1)S(1)}, u32[]{:S(2)}, u32[]{:S(2)}) collective-permute-start(bf16[4,8192]{1,0:T(4,128)(2,1)S(1)} %copy.166), channel_id=1, source_target_pairs={{0,1},{1,2},{2,3},{3,0},{4,5},{5,6},{6,7},{7,4},{8,9},{9,10},{10,1... | collective-permute-start | bytes 196616 | tf_op jit(solution)/shard_map/while/body/eval_jaxpr/ppermute | solution.py:16
  62.3 7.3 %collective-permute-start.2 = (f32[4,64]{1,0:T(4,128)S(1)}, f32[4,64]{1,0:T(4,128)S(1)}, u32[]{:S(2)}, u32[]{:S(2)}) collective-permute-start(f32[4,64]{1,0:T(4,128)S(1)} %get-tuple-element.508), channel_id=1, source_target_pairs={{0,1},{1,2},{2,3},{3,0},{4,5},{5,6},{6,7},{7,4},{8,9},{9,10},{10,1... | collective-permute-start | bytes 3080 | tf_op jit(solution)/shard_map/while/body/eval_jaxpr/ppermute | solution.py:16
  62.9 6.6 %collective-permute-start.3 = (f32[4,64]{1,0:T(4,128)S(1)}, f32[4,64]{1,0:T(4,128)S(1)}, u32[]{:S(2)}, u32[]{:S(2)}) collective-permute-start(f32[4,64]{1,0:T(4,128)S(1)} %get-tuple-element.509), channel_id=1, source_target_pairs={{0,1},{1,2},{2,3},{3,0},{4,5},{5,6},{6,7},{7,4},{8,9},{9,10},{10,1... | collective-permute-start | bytes 3080 | tf_op jit(solution)/shard_map/while/body/eval_jaxpr/ppermute | solution.py:16
  73.7 1.6 %copy-start.1 = (bf16[2048,4,128]{2,1,0:T(4,128)(2,1)S(1)}, bf16[2048,4,128]{2,1,0:T(4,128)(2,1)}, u32[]{:S(2)}) copy-start(bf16[2048,4,128]{2,1,0:T(4,128)(2,1)} %get-tuple-element.553) | copy-start | bytes 6291460 | tf_op jit(solution)/shard_map/while
  76.7 7.6 %collective-permute-start.1 = (f32[4,8192]{1,0:T(4,128)S(1)}, f32[4,8192]{1,0:T(4,128)S(1)}, u32[]{:S(2)}, u32[]{:S(2)}) collective-permute-start(f32[4,8192]{1,0:T(4,128)S(1)} %fusion.71), channel_id=1, source_target_pairs={{0,1},{1,2},{2,3},{3,0},{4,5},{5,6},{6,7},{7,4},{8,9},{9,10},{10,1... | collective-permute-start | bytes 393224 | tf_op jit(solution)/shard_map/while/body/eval_jaxpr/ppermute | solution.py:16
  77.8 6.5 %collective-permute-start = (bf16[4,8192]{1,0:T(4,128)(2,1)S(1)}, bf16[4,8192]{1,0:T(4,128)(2,1)S(1)}, u32[]{:S(2)}, u32[]{:S(2)}) collective-permute-start(bf16[4,8192]{1,0:T(4,128)(2,1)S(1)} %copy.166), channel_id=1, source_target_pairs={{0,1},{1,2},{2,3},{3,0},{4,5},{5,6},{6,7},{7,4},{8,9},{9,10},{10,1... | collective-permute-start | bytes 196616 | tf_op jit(solution)/shard_map/while/body/eval_jaxpr/ppermute | solution.py:16
  77.8 6.4 %collective-permute-start.2 = (f32[4,64]{1,0:T(4,128)S(1)}, f32[4,64]{1,0:T(4,128)S(1)}, u32[]{:S(2)}, u32[]{:S(2)}) collective-permute-start(f32[4,64]{1,0:T(4,128)S(1)} %get-tuple-element.508), channel_id=1, source_target_pairs={{0,1},{1,2},{2,3},{3,0},{4,5},{5,6},{6,7},{7,4},{8,9},{9,10},{10,1... | collective-permute-start | bytes 3080 | tf_op jit(solution)/shard_map/while/body/eval_jaxpr/ppermute | solution.py:16
  78.5 5.8 %collective-permute-start.3 = (f32[4,64]{1,0:T(4,128)S(1)}, f32[4,64]{1,0:T(4,128)S(1)}, u32[]{:S(2)}, u32[]{:S(2)}) collective-permute-start(f32[4,64]{1,0:T(4,128)S(1)} %get-tuple-element.509), channel_id=1, source_target_pairs={{0,1},{1,2},{2,3},{3,0},{4,5},{5,6},{6,7},{7,4},{8,9},{9,10},{10,1... | collective-permute-start | bytes 3080 | tf_op jit(solution)/shard_map/while/body/eval_jaxpr/ppermute | solution.py:16
  88.4 1.6 %copy-start.1 = (bf16[2048,4,128]{2,1,0:T(4,128)(2,1)S(1)}, bf16[2048,4,128]{2,1,0:T(4,128)(2,1)}, u32[]{:S(2)}) copy-start(bf16[2048,4,128]{2,1,0:T(4,128)(2,1)} %get-tuple-element.553) | copy-start | bytes 6291460 | tf_op jit(solution)/shard_map/while
  91.4 7.9 %collective-permute-start.1 = (f32[4,8192]{1,0:T(4,128)S(1)}, f32[4,8192]{1,0:T(4,128)S(1)}, u32[]{:S(2)}, u32[]{:S(2)}) collective-permute-start(f32[4,8192]{1,0:T(4,128)S(1)} %fusion.71), channel_id=1, source_target_pairs={{0,1},{1,2},{2,3},{3,0},{4,5},{5,6},{6,7},{7,4},{8,9},{9,10},{10,1... | collective-permute-start | bytes 393224 | tf_op jit(solution)/shard_map/while/body/eval_jaxpr/ppermute | solution.py:16
  92.5 6.8 %collective-permute-start = (bf16[4,8192]{1,0:T(4,128)(2,1)S(1)}, bf16[4,8192]{1,0:T(4,128)(2,1)S(1)}, u32[]{:S(2)}, u32[]{:S(2)}) collective-permute-start(bf16[4,8192]{1,0:T(4,128)(2,1)S(1)} %copy.166), channel_id=1, source_target_pairs={{0,1},{1,2},{2,3},{3,0},{4,5},{5,6},{6,7},{7,4},{8,9},{9,10},{10,1... | collective-permute-start | bytes 196616 | tf_op jit(solution)/shard_map/while/body/eval_jaxpr/ppermute | solution.py:16
  93.6 5.4 %collective-permute-start.2 = (f32[4,64]{1,0:T(4,128)S(1)}, f32[4,64]{1,0:T(4,128)S(1)}, u32[]{:S(2)}, u32[]{:S(2)}) collective-permute-start(f32[4,64]{1,0:T(4,128)S(1)} %get-tuple-element.508), channel_id=1, source_target_pairs={{0,1},{1,2},{2,3},{3,0},{4,5},{5,6},{6,7},{7,4},{8,9},{9,10},{10,1... | collective-permute-start | bytes 3080 | tf_op jit(solution)/shard_map/while/body/eval_jaxpr/ppermute | solution.py:16
  93.9 5.4 %collective-permute-start.3 = (f32[4,64]{1,0:T(4,128)S(1)}, f32[4,64]{1,0:T(4,128)S(1)}, u32[]{:S(2)}, u32[]{:S(2)}) collective-permute-start(f32[4,64]{1,0:T(4,128)S(1)} %get-tuple-element.509), channel_id=1, source_target_pairs={{0,1},{1,2},{2,3},{3,0},{4,5},{5,6},{6,7},{7,4},{8,9},{9,10},{10,1... | collective-permute-start | bytes 3080 | tf_op jit(solution)/shard_map/while/body/eval_jaxpr/ppermute | solution.py:16
where the time goes:
time: 101 us
  blocking collectives  28.2 us (28%)
  starting transfers between devices  20 us (20%)
  matrix products  13.8 us (14%)
  local copies, waits for them, and re-layouts  13.1 us (13%)
  waiting for transfers between devices  12.9 us (13%)
  other arithmetic  8.9 us (9%)
  loops' own time  3.04 us (3%)
    ppermute x16, starting transfers between devices, from_behind(): lax.ppermute(x, axis, [(i, (i + by) % devices) for i in range(devices)])  20 us
    all_gather x1, blocking collectives, local(): keys_piece = lax.all_gather(new_keys, 'ctx', axis=0, tiled=True)  14.9 us
    all_gather x1, blocking collectives, local(): values_piece = lax.all_gather(new_values, 'ctx', axis=0, tiled=True)  13.3 us
    ppermute x16, waiting for transfers between devices, from_behind(): lax.ppermute(x, axis, [(i, (i + by) % devices) for i in range(devices)])  12.9 us
    dot_general x5, matrix products, attend(): jnp.einsum('rkgd,nkd->rkgn', grouped, keys_grouped, preferred_element_typ...  10.4 us
    while x20, local copies, waits for them, and re-layouts  4.75 us
    reshape x2, local copies, waits for them, and re-layouts, attend(): keys_grouped = keys.reshape(key_count, KVH, HD)  4.13 us
    dot_general x5, matrix products, attend(): jnp.einsum('rkgn,nkd->rkgd', weights.astype(jnp.bfloat16), values_grouped...  3.43 us
  transfers between devices with their start and end apart: 16, of which 6 were waited for; matrix products, arithmetic and copies ran while one was open for 0% of the time, Pallas kernels for 0%

commit v1 on v0

v1 whole, which is shorter than its diff:
```python
import functools
import math

import jax
import jax.numpy as jnp
from jax import lax
from jax.experimental import pallas as pl
from jax.experimental.pallas import tpu as pltpu
from jax.sharding import PartitionSpec as P

HD = 128
PAGE = 128
FLOOR = -1e30
BLOCK = 256


def kernel(
    count,
    q_ref,
    new_k_ref,
    new_v_ref,
    cache_k_ref,
    cache_v_ref,
    length_ref,
    table_ref,
    out_ref,
    new_k,
    new_v,
    length_at,
    table,
    tail,
    q_all,
    k_buf,
    v_buf,
    bias,
    scores,
    part,
    stat,
    part_in,
    stat_in,
    weigh,
    small_sem,
    k_sem,
    v_sem,
    q_send,
    q_recv,
    part_send,
    part_recv,
    stat_send,
    stat_recv,
):
    me = lax.axis_index("ctx")
    kvh, own, _ = q_ref.shape
    rows = new_k_ref.shape[1]
    cached = cache_k_ref.shape[0]
    pages = cached // PAGE
    total_rows = count * own
    block = min(BLOCK, total_rows)
    scale = HD ** (-0.5) * math.log2(math.e)

    def cache_copy(source, target, sems, k):
        return pltpu.make_async_copy(
            source.at[:, pl.ds(k * HD, HD)], target.at[k, pl.ds(0, cached)], sems.at[k]
        )

    barrier = pltpu.get_barrier_semaphore()
    for off in range(1, count):
        pl.semaphore_signal(
            barrier,
            inc=1,
            device_id={"ctx": lax.rem(me + off, count)},
            device_id_type=pl.DeviceIdType.MESH,
        )
    small = [
        pltpu.make_async_copy(source, target, small_sem.at[i])
        for i, (source, target) in enumerate(
            (
                (new_k_ref, new_k),
                (new_v_ref, new_v),
                (length_ref, length_at),
                (table_ref, table),
            )
        )
    ]
    own_q = pltpu.make_async_copy(q_ref, q_all.at[:, me], small_sem.at[len(small)])
    for copy in small:
        copy.start()
    own_q.start()
    for k in range(kvh):
        cache_copy(cache_k_ref, k_buf, k_sem, k).start()
        cache_copy(cache_v_ref, v_buf, v_sem, k).start()
    pl.semaphore_wait(barrier, count - 1)

    def q_copy(k, off):
        return pltpu.make_async_remote_copy(
            src_ref=q_ref.at[k],
            dst_ref=q_all.at[k, me],
            send_sem=q_send.at[k, off - 1],
            recv_sem=q_recv.at[k, off - 1],
            device_id={"ctx": lax.rem(me + off, count)},
            device_id_type=pl.DeviceIdType.MESH,
        )

    def part_copy(k, off):
        target = lax.rem(me + off, count)
        return pltpu.make_async_remote_copy(
            src_ref=part.at[k, target],
            dst_ref=part_in.at[k, me],
            send_sem=part_send.at[k, off - 1],
            recv_sem=part_recv.at[k, off - 1],
            device_id={"ctx": target},
            device_id_type=pl.DeviceIdType.MESH,
        )

    def stat_copy(k, off):
        target = lax.rem(me + off, count)
        return pltpu.make_async_remote_copy(
            src_ref=stat.at[k, target],
            dst_ref=stat_in.at[k, me],
            send_sem=stat_send.at[k, off - 1],
            recv_sem=stat_recv.at[k, off - 1],
            device_id={"ctx": target},
            device_id_type=pl.DeviceIdType.MESH,
        )

    for k in range(kvh):
        for off in range(1, count):
            q_copy(k, off).start()

    for copy in small:
        copy.wait()
    tail[...] = jnp.zeros_like(tail)
    for k in range(kvh):
        tail[0:rows, :] = new_k[k].astype(jnp.float32)
        k_buf[k, cached:, :] = tail[...].astype(jnp.bfloat16)
        tail[0:rows, :] = new_v[k].astype(jnp.float32)
        v_buf[k, cached:, :] = tail[...].astype(jnp.bfloat16)

    length = length_at[0]
    slots = me * pages + lax.broadcasted_iota(jnp.int32, (pages, table.shape[1]), 0)
    order = lax.broadcasted_iota(jnp.int32, (pages, table.shape[1]), 1)
    hits = jnp.where(table[...] == slots, order, 0)
    logical = jnp.sum(hits, axis=1, keepdims=True)
    lane = lax.broadcasted_iota(jnp.int32, (pages, PAGE), 1)
    bias[...] = jnp.where(logical * PAGE + lane < length, 0.0, FLOOR)

    spans = [(at, min(BLOCK, cached - at)) for at in range(0, cached, BLOCK)]

    def attend(k, at):
        if total_rows == block:
            query = q_all[k].reshape(total_rows, HD)
        else:
            parts = block // own
            query = q_all[k, pl.ds(at * parts, parts)].reshape(block, HD)
        top = None
        for start, size in spans:
            score = lax.dot_general(
                query,
                k_buf[k, start : start + size, :],
                (((1,), (1,)), ((), ())),
                preferred_element_type=jnp.float32,
            )
            for page in range(size // PAGE):
                j = start // PAGE + page
                tile = score[:, page * PAGE : (page + 1) * PAGE] * scale + bias[j : j + 1, :]
                scores[:, j * PAGE : (j + 1) * PAGE] = tile
                top = tile if top is None else jnp.maximum(top, tile)
        score = lax.dot_general(
            query,
            k_buf[k, cached:, :],
            (((1,), (1,)), ((), ())),
            preferred_element_type=jnp.float32,
        )
        row = at * block + lax.broadcasted_iota(jnp.int32, (block, PAGE), 0)
        column = lax.broadcasted_iota(jnp.int32, (block, PAGE), 1)
        token = (row // own) * rows + row % rows
        allowed = (column < rows) & (me * rows + column <= token)
        last = jnp.where(allowed, score * scale, FLOOR)
        top = jnp.max(jnp.maximum(top, last), axis=1, keepdims=True)
        weight = jnp.exp2(last - top)
        summed = weight
        mixed = jnp.dot(
            weight.astype(jnp.bfloat16), v_buf[k, cached:, :], preferred_element_type=jnp.float32
        )
        for start, size in spans:
            weight = jnp.exp2(scores[:, start : start + size] - top)
            for page in range(size // PAGE):
                summed = summed + weight[:, page * PAGE : (page + 1) * PAGE]
            mixed = mixed + jnp.dot(
                weight.astype(jnp.bfloat16),
                v_buf[k, start : start + size, :],
                preferred_element_type=jnp.float32,
            )
        total = jnp.sum(summed, axis=1, keepdims=True)
        mixed = mixed * (1.0 / total)
        lanes = lax.broadcasted_iota(jnp.int32, (2 * own, 128), 1)
        columns = jnp.zeros((2 * own, 128), jnp.float32)
        for i in range(block // own):
            piece = slice(i * own, (i + 1) * own)
            slot = at * (block // own) + i
            part[k, slot] = mixed[piece].astype(jnp.bfloat16)
            column = jnp.concatenate([top[piece], total[piece]], axis=0)
            columns = jnp.where(lanes == i, column, columns)
        turned = columns.T
        for i in range(block // own):
            stat[k, at * (block // own) + i] = turned[i : i + 1, :]

    own_q.wait()

    def one_head(k, carry):
        for off in range(1, count):
            q_copy(k, off).wait_recv()
        cache_copy(cache_k_ref, k_buf, k_sem, k).wait()
        cache_copy(cache_v_ref, v_buf, v_sem, k).wait()
        if total_rows == block:
            attend(k, 0)
        else:
            lax.fori_loop(0, total_rows // block, lambda at, c: (attend(k, at), c)[1], 0)
        for off in range(1, count):
            part_copy(k, off).start()
            stat_copy(k, off).start()
        part_in[k, me] = part[k, me]
        stat_in[k, me] = stat[k, me]
        return carry

    lax.fori_loop(0, kvh, one_head, 0)

    def combine(k, carry):
        for off in range(1, count):
            part_copy(k, off).wait_recv()
            stat_copy(k, off).wait_recv()
        tops = [stat_in[k, s] for s in range(count)]
        totals = [pltpu.roll(t, own, 1) for t in tops]
        top = functools.reduce(jnp.maximum, tops)
        shares = [jnp.exp2(t - top) * l for t, l in zip(tops, totals)]
        share = 1.0 / functools.reduce(jnp.add, shares)
        for s in range(count):
            weigh[s : s + 1, :] = shares[s] * share
        turned = weigh[...].T
        result = jnp.zeros((own, HD), jnp.float32)
        for s in range(count):
            result = result + part_in[k, s].astype(jnp.float32) * turned[0:own, s : s + 1]
        out_ref[k] = result.astype(out_ref.dtype)
        return carry

    weigh[...] = jnp.zeros_like(weigh)
    lax.fori_loop(0, kvh, combine, 0)

    for k in range(kvh):
        for off in range(1, count):
            q_copy(k, off).wait_send()
            part_copy(k, off).wait_send()
            stat_copy(k, off).wait_send()


def local(queries, new_keys, new_values, cache_keys, cache_values, cache_length, page_table):
    count = lax.axis_size("ctx")
    rows, width = queries.shape
    heads = width // HD
    cached = cache_keys.shape[0]
    kvh = cache_keys.shape[1] // HD
    group = heads // kvh
    own = rows * group
    block = min(BLOCK, count * own)
    pages = cached // PAGE
    vmem = pl.BlockSpec(memory_space=pltpu.VMEM)
    held = pl.BlockSpec(memory_space=pl.ANY)
    dma = pltpu.SemaphoreType.DMA
    out = pl.pallas_call(
        functools.partial(kernel, count),
        out_shape=jax.ShapeDtypeStruct((kvh, own, HD), jnp.bfloat16),
        in_specs=[held] * 7,
        out_specs=vmem,
        scratch_shapes=[
            pltpu.VMEM((kvh, rows, HD), jnp.bfloat16),
            pltpu.VMEM((kvh, rows, HD), jnp.bfloat16),
            pltpu.SMEM((1,), jnp.int32),
            pltpu.VMEM((1, page_table.shape[0]), jnp.int32),
            pltpu.VMEM((PAGE, HD), jnp.float32),
            pltpu.VMEM((kvh, count, own, HD), jnp.bfloat16),
            pltpu.VMEM((kvh, cached + PAGE, HD), jnp.bfloat16),
            pltpu.VMEM((kvh, cached + PAGE, HD), jnp.bfloat16),
            pltpu.VMEM((pages, PAGE), jnp.float32),
            pltpu.VMEM((block, cached), jnp.float32),
            pltpu.VMEM((kvh, count, own, HD), jnp.bfloat16),
            pltpu.VMEM((kvh, count, 1, 2 * own), jnp.float32),
            pltpu.VMEM((kvh, count, own, HD), jnp.bfloat16),
            pltpu.VMEM((kvh, count, 1, 2 * own), jnp.float32),
            pltpu.VMEM((128, 2 * own), jnp.float32),
            dma((5,)),
            dma((kvh,)),
            dma((kvh,)),
            dma((kvh, count - 1)),
            dma((kvh, count - 1)),
            dma((kvh, count - 1)),
            dma((kvh, count - 1)),
            dma((kvh, count - 1)),
            dma((kvh, count - 1)),
        ],
        compiler_params=pltpu.CompilerParams(
            collective_id=0, has_side_effects=True, vmem_limit_bytes=60 * 1024 * 1024
        ),
        cost_estimate=pl.CostEstimate(
            flops=4 * count * rows * heads * cached * HD,
            bytes_accessed=4 * cached * kvh * HD,
            transcendentals=count * rows * heads * cached,
        ),
        name="paged_attention",
    )(
        queries.reshape(rows, heads, HD).transpose(1, 0, 2).reshape(kvh, own, HD),
        new_keys.reshape(rows, kvh, HD).transpose(1, 0, 2),
        new_values.reshape(rows, kvh, HD).transpose(1, 0, 2),
        cache_keys,
        cache_values,
        cache_length,
        page_table.reshape(1, -1),
    )
    return out.reshape(heads, rows, HD).transpose(1, 0, 2).reshape(rows, width)


def solution(mesh):
    in_specs = (
        P(("req", "ctx"), None),
        P(("req", "ctx"), None),
        P(("req", "ctx"), None),
        P(("req", "ctx"), None),
        P(("req", "ctx"), None),
        P("req"),
        P("req"),
    )
    out_specs = P(("req", "ctx"), None)
    return jax.shard_map(local, mesh=mesh, in_specs=in_specs, out_specs=out_specs, check_vma=False)
```

time: 101 us -> 23.3 us (0.23)
  blocking collectives: 28.2 us -> 0 us
  Pallas kernels: 0 us -> 21 us
  starting transfers between devices: 20 us -> 0 us
  matrix products: 13.8 us -> 0 us
  waiting for transfers between devices: 12.9 us -> 0 us
  local copies, waits for them, and re-layouts: 13.1 us -> 1.49 us
  other arithmetic: 8.9 us -> 0 us
  loops' own time: 3.04 us -> 0 us
    all_gather x2 -> x0, blocking collectives: 28.2 us -> none  [the longest x1 14.9 us: local(): keys_piece = lax.all_gather(new_keys, 'ctx', axis=0, tiled=True)]
    pallas_call x0 -> x1, Pallas kernels: none -> 21 us  [local(): pl.pallas_call(functools.partial(kernel, count), out_shape=jax.ShapeDtype...]
    ppermute x16 -> x0, starting transfers between devices: 20 us -> none  [from_behind(): lax.ppermute(x, axis, [(i, (i + by) % devices) for i in range(devices)])]
    dot_general x10 -> x0, matrix products: 13.8 us -> none  [the longest x5 10.4 us: attend(): jnp.einsum('rkgd,nkd->rkgn', grouped, keys_grouped, preferred_element_typ...]
    ppermute x16 -> x0, waiting for transfers between devices: 12.9 us -> none  [from_behind(): lax.ppermute(x, axis, [(i, (i + by) % devices) for i in range(devices)])]
    reshape x14 -> x0, local copies, waits for them, and re-layouts: 7.03 us -> none  [the longest x2 4.13 us: attend(): keys_grouped = keys.reshape(key_count, KVH, HD)]
    while x20 -> x0, local copies, waits for them, and re-layouts: 4.75 us -> none
    reduce_sum x6 -> x0, other arithmetic: 3.16 us -> none  [the longest x5 2.32 us: attend(): total = jnp.sum(weights, axis=3)]
  transfers between devices with their start and end apart: 16 -> 0, of which waited for: 6 -> 0; matrix products, arithmetic and copies ran while one was open for 0% -> 0% of each run, Pallas kernels for 0% -> 0%
where the time goes in v1:
time: 23.3 us; the launch traced here: 23.2 us
  Pallas kernels  21 us (90%)
  local copies, waits for them, and re-layouts  1.49 us (6%)
  between operations  0.66 us (3%)
    pallas_call x1, Pallas kernels, local(): pl.pallas_call(functools.partial(kernel, count), out_shape=jax.ShapeDtype...  21 us
    unnamed x1, local copies, waits for them, and re-layouts  1.49 us

profile of v1, /device:TPU:0, one launch (start us, length us, event | category | flops | bytes accessed | tf_op | source)
XLA Modules:
  0.0 23.2 jit_solution(8815316512275956210)
XLA Ops:
  0.7 21.0 %paged_attention.1 = bf16[4,64,128]{2,1,0:T(8,128)(2,1)} custom-call(bf16[4,64,128]{2,1,0:T(8,128)(2,1)} %bitcast.18, bf16[4,4,128]{2,1,0:T(4,128)(2,1)} %bitcast.19, bf16[4,4,128]{2,1,0:T(4,128)(2,1)} %bitcast.20, bf16[2048,512]{1,0:T(8,128)(2,1)} %cache_k_ref.1, bf16[2048,512]{1,0:T(8,128)(2,1)} %cache_v_ref.1, s32[1]{0:T(128)S(6)} %copy.11.length_ref, ...), custom_call_target="tpu_custom_call" | custom-call | flops 1073741824 | bytes 4194304 | tf_op jit(solution)/shard_map/paged_attention/pallas_call | solution.py:269
  21.7 1.5 %copy.12 = bf16[4,8192]{1,0:T(4,128)(2,1)} copy(bf16[4,8192]{1,0:T(4,128)(2,1)} %bitcast.17) | data formatting | bytes 131072

commit v2 on v1

--- a/solution.py
+++ b/solution.py
@@ -264,11 +264,11 @@
     block = min(BLOCK, count * own)
     pages = cached // PAGE
     vmem = pl.BlockSpec(memory_space=pltpu.VMEM)
-    held = pl.BlockSpec(memory_space=pl.ANY)
+    held = pl.BlockSpec(memory_space=pltpu.HBM)
     dma = pltpu.SemaphoreType.DMA
     out = pl.pallas_call(
         functools.partial(kernel, count),
-        out_shape=jax.ShapeDtypeStruct((kvh, own, HD), jnp.bfloat16),
+        out_shape=pltpu.VMEM((kvh, own, HD), jnp.bfloat16),
         in_specs=[held] * 7,
         out_specs=vmem,
         scratch_shapes=[

time: 23.3 us -> 21.9 us (0.940)
  local copies, waits for them, and re-layouts: 1.49 us -> 0.63 us
  Pallas kernels: 21 us -> 20.4 us
    unnamed x1, local copies, waits for them, and re-layouts: 1.49 us -> 0.63 us
    pallas_call x1, Pallas kernels: 21 us -> 20.4 us  [local(): pl.pallas_call(functools.partial(kernel, count), out_shape=pltpu.VMEM((kv...]
where the time goes in v2:
time: 21.9 us; the launch traced here: 21.7 us
  Pallas kernels  20.4 us (93%)
  between operations  0.66 us (3%)
  local copies, waits for them, and re-layouts  0.63 us (3%)
    pallas_call x1, Pallas kernels, local(): pl.pallas_call(functools.partial(kernel, count), out_shape=pltpu.VMEM((kv...  20.4 us
    unnamed x1, local copies, waits for them, and re-layouts  0.63 us

profile of v2, /device:TPU:0, one launch (start us, length us, event | category | flops | bytes accessed | tf_op | source)
XLA Modules:
  0.0 21.7 jit_solution(2024129236434091934)
XLA Ops:
  0.7 20.4 %paged_attention.1 = bf16[4,64,128]{2,1,0:T(8,128)(2,1)S(1)} custom-call(bf16[4,64,128]{2,1,0:T(8,128)(2,1)} %bitcast.18, bf16[4,4,128]{2,1,0:T(4,128)(2,1)} %bitcast.19, bf16[4,4,128]{2,1,0:T(4,128)(2,1)} %bitcast.20, bf16[2048,512]{1,0:T(8,128)(2,1)} %cache_k_ref.1, bf16[2048,512]{1,0:T(8,128)(2,1)} %cache_v_ref.1, s32[1]{0:T(128)S(6)} %copy.12.length_ref, ...), custom_call_target="tpu_custom_call" | custom-call | flops 1073741824 | bytes 4194304 | tf_op jit(solution)/shard_map/paged_attention/pallas_call | solution.py:269
  21.1 0.6 %copy.11 = bf16[4,8192]{1,0:T(4,128)(2,1)} copy(bf16[4,8192]{1,0:T(4,128)(2,1)S(1)} %bitcast.17) | data formatting | bytes 131072

commit v3 on v2

--- a/solution.py
+++ b/solution.py
@@ -44,6 +44,10 @@
     v_sem,
     q_send,
     q_recv,
+    cross_send,
+    cross_recv,
+    pass_send,
+    pass_recv,
     part_send,
     part_recv,
     stat_send,
@@ -91,15 +95,51 @@
         cache_copy(cache_v_ref, v_buf, v_sem, k).start()
     pl.semaphore_wait(barrier, count - 1)
 
+    halves = 2 if count % 2 == 0 else 1
+    half = count // halves
+    side = me // half
+    base = side * half
+    other = (halves - 1 - side) * half
+    relay = me == half - 1 + side
+
+    def near(off):
+        return base + lax.rem(me - base + off, half)
+
     def q_copy(k, off):
         return pltpu.make_async_remote_copy(
             src_ref=q_ref.at[k],
             dst_ref=q_all.at[k, me],
             send_sem=q_send.at[k, off - 1],
             recv_sem=q_recv.at[k, off - 1],
-            device_id={"ctx": lax.rem(me + off, count)},
-            device_id_type=pl.DeviceIdType.MESH,
-        )
+            device_id={"ctx": near(off)},
+            device_id_type=pl.DeviceIdType.MESH,
+        )
+
+    def cross_copy(k, slot):
+        return pltpu.make_async_remote_copy(
+            src_ref=q_ref.at[k],
+            dst_ref=q_all.at[k, me],
+            send_sem=cross_send.at[k],
+            recv_sem=cross_recv.at[k, slot],
+            device_id={"ctx": half - side},
+            device_id_type=pl.DeviceIdType.MESH,
+        )
+
+    def pass_copy(k, off):
+        return pltpu.make_async_remote_copy(
+            src_ref=q_all.at[k, pl.ds(other, half)],
+            dst_ref=q_all.at[k, pl.ds(other, half)],
+            send_sem=pass_send.at[k, off - 1],
+            recv_sem=pass_recv.at[k],
+            device_id={"ctx": near(off)},
+            device_id_type=pl.DeviceIdType.MESH,
+        )
+
+    def pass_on(k):
+        for slot in range(half):
+            cross_copy(k, slot).wait_recv()
+        for off in range(1, half):
+            pass_copy(k, off).start()
 
     def part_copy(k, off):
         target = lax.rem(me + off, count)
@@ -124,7 +164,9 @@
         )
 
     for k in range(kvh):
-        for off in range(1, count):
+        if halves == 2:
+            cross_copy(k, me - base).start()
+        for off in range(1, half):
             q_copy(k, off).start()
 
     for copy in small:
@@ -146,7 +188,7 @@
 
     spans = [(at, min(BLOCK, cached - at)) for at in range(0, cached, BLOCK)]
 
-    def attend(k, at):
+    def attend(k, at, between=None):
         if total_rows == block:
             query = q_all[k].reshape(total_rows, HD)
         else:
@@ -171,6 +213,8 @@
             (((1,), (1,)), ((), ())),
             preferred_element_type=jnp.float32,
         )
+        if between is not None:
+            between()
         row = at * block + lax.broadcasted_iota(jnp.int32, (block, PAGE), 0)
         column = lax.broadcasted_iota(jnp.int32, (block, PAGE), 1)
         token = (row // own) * rows + row % rows
@@ -206,15 +250,28 @@
             stat[k, at * (block // own) + i] = turned[i : i + 1, :]
 
     own_q.wait()
+    if halves == 2:
+        pl.when(relay)(lambda: pass_on(0))
+
+    def pass_next(k):
+        if halves == 2:
+            pl.when(relay & (k + 1 < kvh))(lambda: pass_on(k + 1))
 
     def one_head(k, carry):
-        for off in range(1, count):
+        for off in range(1, half):
             q_copy(k, off).wait_recv()
+        if halves == 2 and half > 1:
+
+            @pl.when(jnp.logical_not(relay))
+            def _():
+                pass_copy(k, 1).wait_recv()
+
         cache_copy(cache_k_ref, k_buf, k_sem, k).wait()
         cache_copy(cache_v_ref, v_buf, v_sem, k).wait()
         if total_rows == block:
-            attend(k, 0)
+            attend(k, 0, lambda: pass_next(k))
         else:
+            pass_next(k)
             lax.fori_loop(0, total_rows // block, lambda at, c: (attend(k, at), c)[1], 0)
         for off in range(1, count):
             part_copy(k, off).start()
@@ -247,10 +304,20 @@
     lax.fori_loop(0, kvh, combine, 0)
 
     for k in range(kvh):
+        for off in range(1, half):
+            q_copy(k, off).wait_send()
         for off in range(1, count):
-            q_copy(k, off).wait_send()
             part_copy(k, off).wait_send()
             stat_copy(k, off).wait_send()
+    if halves == 2:
+        for k in range(kvh):
+            cross_copy(k, 0).wait_send()
+
+        @pl.when(relay)
+        def _():
+            for k in range(kvh):
+                for off in range(1, half):
+                    pass_copy(k, off).wait_send()
 
 
 def local(queries, new_keys, new_values, cache_keys, cache_values, cache_length, page_table):
@@ -263,6 +330,7 @@
     own = rows * group
     block = min(BLOCK, count * own)
     pages = cached // PAGE
+    half = count // 2 if count % 2 == 0 else count
     vmem = pl.BlockSpec(memory_space=pltpu.VMEM)
     held = pl.BlockSpec(memory_space=pltpu.HBM)
     dma = pltpu.SemaphoreType.DMA
@@ -290,8 +358,12 @@
             dma((5,)),
             dma((kvh,)),
             dma((kvh,)),
-            dma((kvh, count - 1)),
-            dma((kvh, count - 1)),
+            dma((kvh, max(half - 1, 1))),
+            dma((kvh, max(half - 1, 1))),
+            dma((kvh,)),
+            dma((kvh, half)),
+            dma((kvh, max(half - 1, 1))),
+            dma((kvh,)),
             dma((kvh, count - 1)),
             dma((kvh, count - 1)),
             dma((kvh, count - 1)),

time: 21.9 us -> 23.2 us (1.059)
  Pallas kernels: 20.4 us -> 21.8 us
    pallas_call x1, Pallas kernels: 20.4 us -> 21.8 us  [local(): pl.pallas_call(functools.partial(kernel, count), out_shape=pltpu.VMEM((kv...]
where the time goes in v3:
time: 23.2 us; the launch traced here: 23.1 us
  Pallas kernels  21.8 us (94%)
  between operations  0.66 us (3%)
  local copies, waits for them, and re-layouts  0.63 us (3%)
    pallas_call x1, Pallas kernels, local(): pl.pallas_call(functools.partial(kernel, count), out_shape=pltpu.VMEM((kv...  21.8 us
    unnamed x1, local copies, waits for them, and re-layouts  0.63 us

profile of v3, /device:TPU:0, one launch (start us, length us, event | category | flops | bytes accessed | tf_op | source)
XLA Modules:
  0.0 23.1 jit_solution(12200758871282273385)
XLA Ops:
  0.7 21.8 %paged_attention.1 = bf16[4,64,128]{2,1,0:T(8,128)(2,1)S(1)} custom-call(bf16[4,64,128]{2,1,0:T(8,128)(2,1)} %bitcast.18, bf16[4,4,128]{2,1,0:T(4,128)(2,1)} %bitcast.19, bf16[4,4,128]{2,1,0:T(4,128)(2,1)} %bitcast.20, bf16[2048,512]{1,0:T(8,128)(2,1)} %cache_k_ref.1, bf16[2048,512]{1,0:T(8,128)(2,1)} %cache_v_ref.1, s32[1]{0:T(128)S(6)} %copy.12.length_ref, ...), custom_call_target="tpu_custom_call" | custom-call | flops 1073741824 | bytes 4194304 | tf_op jit(solution)/shard_map/paged_attention/pallas_call | solution.py:337
  22.4 0.6 %copy.11 = bf16[4,8192]{1,0:T(4,128)(2,1)} copy(bf16[4,8192]{1,0:T(4,128)(2,1)S(1)} %bitcast.17) | data formatting | bytes 131072

commit v4 on v2

--- a/solution.py
+++ b/solution.py
@@ -30,10 +30,13 @@
     table,
     tail,
     q_all,
+    q_mark,
     k_buf,
+    k_mark,
     v_buf,
-    bias,
+    pages_at,
     scores,
+    weights,
     part,
     stat,
     part_in,
@@ -136,74 +139,73 @@
         tail[0:rows, :] = new_v[k].astype(jnp.float32)
         v_buf[k, cached:, :] = tail[...].astype(jnp.bfloat16)
 
+    mark = q_mark.shape[1]
+    row = lax.broadcasted_iota(jnp.int32, (total_rows, mark), 0)
+    column = lax.broadcasted_iota(jnp.int32, (total_rows, mark), 1)
+    token = (row // own) * rows + row % rows
+    chosen = (column == 0) | (column == token + 1)
+    q_mark[...] = jnp.where(chosen, 1.0, 0.0).astype(jnp.bfloat16)
+
     length = length_at[0]
     slots = me * pages + lax.broadcasted_iota(jnp.int32, (pages, table.shape[1]), 0)
     order = lax.broadcasted_iota(jnp.int32, (pages, table.shape[1]), 1)
-    hits = jnp.where(table[...] == slots, order, 0)
-    logical = jnp.sum(hits, axis=1, keepdims=True)
-    lane = lax.broadcasted_iota(jnp.int32, (pages, PAGE), 1)
-    bias[...] = jnp.where(logical * PAGE + lane < length, 0.0, FLOOR)
-
-    spans = [(at, min(BLOCK, cached - at)) for at in range(0, cached, BLOCK)]
+    logical = jnp.sum(jnp.where(table[...] == slots, order, 0), axis=1, keepdims=True)
+    pages_at[...] = jnp.broadcast_to(logical * PAGE, pages_at.shape)
+    row = lax.broadcasted_iota(jnp.int32, (PAGE, mark), 0)
+    column = lax.broadcasted_iota(jnp.int32, (PAGE, mark), 1)
+    for j in range(pages):
+        dead = (pages_at[j : j + 1, :] + row >= length) & (column == 0)
+        k_mark[j * PAGE : (j + 1) * PAGE, :] = jnp.where(dead, FLOOR, 0.0).astype(jnp.bfloat16)
+    later = (column > 0) & (column <= me * rows + row)
+    dead = ((row < rows) & later) | ((row >= rows) & (column == 0))
+    k_mark[cached:, :] = jnp.where(dead, FLOOR, 0.0).astype(jnp.bfloat16)
+
+    keys = cached + PAGE
+    spans = [(at, min(BLOCK, keys - at)) for at in range(0, keys, BLOCK)]
+    parts = block // own
 
     def attend(k, at):
-        if total_rows == block:
-            query = q_all[k].reshape(total_rows, HD)
-        else:
-            parts = block // own
-            query = q_all[k, pl.ds(at * parts, parts)].reshape(block, HD)
+        query = jnp.concatenate(
+            [
+                q_all[k, pl.ds(at * parts, parts)].reshape(block, HD),
+                q_mark[pl.ds(at * block, block), :],
+            ],
+            axis=1,
+        )
         top = None
         for start, size in spans:
+            span = slice(start, start + size)
             score = lax.dot_general(
                 query,
-                k_buf[k, start : start + size, :],
+                jnp.concatenate([k_buf[k, span, :], k_mark[span, :]], axis=1),
                 (((1,), (1,)), ((), ())),
                 preferred_element_type=jnp.float32,
             )
+            scores[:, span] = score
             for page in range(size // PAGE):
-                j = start // PAGE + page
-                tile = score[:, page * PAGE : (page + 1) * PAGE] * scale + bias[j : j + 1, :]
-                scores[:, j * PAGE : (j + 1) * PAGE] = tile
+                tile = score[:, page * PAGE : (page + 1) * PAGE]
                 top = tile if top is None else jnp.maximum(top, tile)
-        score = lax.dot_general(
-            query,
-            k_buf[k, cached:, :],
-            (((1,), (1,)), ((), ())),
+        top = jnp.max(top, axis=1, keepdims=True)
+        for start, size in spans:
+            span = slice(start, start + size)
+            weights[:, span] = jnp.exp2((scores[:, span] - top) * scale).astype(jnp.bfloat16)
+        mixed = jnp.dot(
+            weights[...],
+            jnp.concatenate([v_buf[k], jnp.ones((keys, HD), jnp.bfloat16)], axis=1),
             preferred_element_type=jnp.float32,
         )
-        row = at * block + lax.broadcasted_iota(jnp.int32, (block, PAGE), 0)
-        column = lax.broadcasted_iota(jnp.int32, (block, PAGE), 1)
-        token = (row // own) * rows + row % rows
-        allowed = (column < rows) & (me * rows + column <= token)
-        last = jnp.where(allowed, score * scale, FLOOR)
-        top = jnp.max(jnp.maximum(top, last), axis=1, keepdims=True)
-        weight = jnp.exp2(last - top)
-        summed = weight
-        mixed = jnp.dot(
-            weight.astype(jnp.bfloat16), v_buf[k, cached:, :], preferred_element_type=jnp.float32
-        )
-        for start, size in spans:
-            weight = jnp.exp2(scores[:, start : start + size] - top)
-            for page in range(size // PAGE):
-                summed = summed + weight[:, page * PAGE : (page + 1) * PAGE]
-            mixed = mixed + jnp.dot(
-                weight.astype(jnp.bfloat16),
-                v_buf[k, start : start + size, :],
-                preferred_element_type=jnp.float32,
-            )
-        total = jnp.sum(summed, axis=1, keepdims=True)
-        mixed = mixed * (1.0 / total)
-        lanes = lax.broadcasted_iota(jnp.int32, (2 * own, 128), 1)
-        columns = jnp.zeros((2 * own, 128), jnp.float32)
-        for i in range(block // own):
+        total = mixed[:, HD:]
+        mixed = mixed[:, :HD] * (1.0 / total)
+        level = top * scale + jnp.log(total) * math.log2(math.e)
+        lanes = lax.broadcasted_iota(jnp.int32, (own, HD), 1)
+        columns = jnp.zeros((own, HD), jnp.float32)
+        for i in range(parts):
             piece = slice(i * own, (i + 1) * own)
-            slot = at * (block // own) + i
-            part[k, slot] = mixed[piece].astype(jnp.bfloat16)
-            column = jnp.concatenate([top[piece], total[piece]], axis=0)
-            columns = jnp.where(lanes == i, column, columns)
+            part[k, at * parts + i] = mixed[piece].astype(jnp.bfloat16)
+            columns = jnp.where(lanes == i, level[piece], columns)
         turned = columns.T
-        for i in range(block // own):
-            stat[k, at * (block // own) + i] = turned[i : i + 1, :]
+        for i in range(parts):
+            stat[k, at * parts + i] = turned[i : i + 1, :]
 
     own_q.wait()
 
@@ -229,17 +231,16 @@
         for off in range(1, count):
             part_copy(k, off).wait_recv()
             stat_copy(k, off).wait_recv()
-        tops = [stat_in[k, s] for s in range(count)]
-        totals = [pltpu.roll(t, own, 1) for t in tops]
-        top = functools.reduce(jnp.maximum, tops)
-        shares = [jnp.exp2(t - top) * l for t, l in zip(tops, totals)]
+        levels = [stat_in[k, s] for s in range(count)]
+        top = functools.reduce(jnp.maximum, levels)
+        shares = [jnp.exp2(level - top) for level in levels]
         share = 1.0 / functools.reduce(jnp.add, shares)
         for s in range(count):
             weigh[s : s + 1, :] = shares[s] * share
         turned = weigh[...].T
         result = jnp.zeros((own, HD), jnp.float32)
         for s in range(count):
-            result = result + part_in[k, s].astype(jnp.float32) * turned[0:own, s : s + 1]
+            result = result + part_in[k, s].astype(jnp.float32) * turned[:, s : s + 1]
         out_ref[k] = result.astype(out_ref.dtype)
         return carry
 
@@ -263,6 +264,7 @@
     own = rows * group
     block = min(BLOCK, count * own)
     pages = cached // PAGE
+    mark = -(-(1 + count * rows) // HD) * HD
     vmem = pl.BlockSpec(memory_space=pltpu.VMEM)
     held = pl.BlockSpec(memory_space=pltpu.HBM)
     dma = pltpu.SemaphoreType.DMA
@@ -278,15 +280,18 @@
             pltpu.VMEM((1, page_table.shape[0]), jnp.int32),
             pltpu.VMEM((PAGE, HD), jnp.float32),
             pltpu.VMEM((kvh, count, own, HD), jnp.bfloat16),
+            pltpu.VMEM((count * own, mark), jnp.bfloat16),
             pltpu.VMEM((kvh, cached + PAGE, HD), jnp.bfloat16),
+            pltpu.VMEM((cached + PAGE, mark), jnp.bfloat16),
             pltpu.VMEM((kvh, cached + PAGE, HD), jnp.bfloat16),
-            pltpu.VMEM((pages, PAGE), jnp.float32),
-            pltpu.VMEM((block, cached), jnp.float32),
+            pltpu.VMEM((pages, mark), jnp.int32),
+            pltpu.VMEM((block, cached + PAGE), jnp.float32),
+            pltpu.VMEM((block, cached + PAGE), jnp.bfloat16),
             pltpu.VMEM((kvh, count, own, HD), jnp.bfloat16),
-            pltpu.VMEM((kvh, count, 1, 2 * own), jnp.float32),
+            pltpu.VMEM((kvh, count, 1, own), jnp.float32),
             pltpu.VMEM((kvh, count, own, HD), jnp.bfloat16),
-            pltpu.VMEM((kvh, count, 1, 2 * own), jnp.float32),
-            pltpu.VMEM((128, 2 * own), jnp.float32),
+            pltpu.VMEM((kvh, count, 1, own), jnp.float32),
+            pltpu.VMEM((HD, own), jnp.float32),
             dma((5,)),
             dma((kvh,)),
             dma((kvh,)),

time: 21.9 us -> 22.7 us (1.037)
  Pallas kernels: 20.4 us -> 21.2 us
    pallas_call x1, Pallas kernels: 20.4 us -> 21.2 us  [local(): pl.pallas_call(functools.partial(kernel, count), out_shape=pltpu.VMEM((kv...]
where the time goes in v4:
time: 22.7 us; the launch traced here: 22.5 us
  Pallas kernels  21.2 us (93%)
  between operations  0.66 us (3%)
  local copies, waits for them, and re-layouts  0.63 us (3%)
    pallas_call x1, Pallas kernels, local(): pl.pallas_call(functools.partial(kernel, count), out_shape=pltpu.VMEM((kv...  21.2 us
    unnamed x1, local copies, waits for them, and re-layouts  0.63 us

profile of v4, /device:TPU:0, one launch (start us, length us, event | category | flops | bytes accessed | tf_op | source)
XLA Modules:
  0.0 22.5 jit_solution(15710341520879273556)
XLA Ops:
  0.7 21.2 %paged_attention.1 = bf16[4,64,128]{2,1,0:T(8,128)(2,1)S(1)} custom-call(bf16[4,64,128]{2,1,0:T(8,128)(2,1)} %bitcast.18, bf16[4,4,128]{2,1,0:T(4,128)(2,1)} %bitcast.19, bf16[4,4,128]{2,1,0:T(4,128)(2,1)} %bitcast.20, bf16[2048,512]{1,0:T(8,128)(2,1)} %cache_k_ref.1, bf16[2048,512]{1,0:T(8,128)(2,1)} %cache_v_ref.1, s32[1]{0:T(128)S(6)} %copy.12.length_ref, ...), custom_call_target="tpu_custom_call" | custom-call | flops 1073741824 | bytes 4194304 | tf_op jit(solution)/shard_map/paged_attention/pallas_call | solution.py:271
  21.9 0.6 %copy.11 = bf16[4,8192]{1,0:T(4,128)(2,1)} copy(bf16[4,8192]{1,0:T(4,128)(2,1)S(1)} %bitcast.17) | data formatting | bytes 131072

commit v5 on v2

--- a/solution.py
+++ b/solution.py
@@ -31,9 +31,11 @@
     tail,
     q_all,
     k_buf,
+    k_turned,
     v_buf,
     bias,
     scores,
+    tops,
     part,
     stat,
     part_in,
@@ -88,6 +90,7 @@
     own_q.start()
     for k in range(kvh):
         cache_copy(cache_k_ref, k_buf, k_sem, k).start()
+    for k in range(kvh):
         cache_copy(cache_v_ref, v_buf, v_sem, k).start()
     pl.semaphore_wait(barrier, count - 1)
 
@@ -144,113 +147,123 @@
     lane = lax.broadcasted_iota(jnp.int32, (pages, PAGE), 1)
     bias[...] = jnp.where(logical * PAGE + lane < length, 0.0, FLOOR)
 
-    spans = [(at, min(BLOCK, cached - at)) for at in range(0, cached, BLOCK)]
-
-    def attend(k, at):
-        if total_rows == block:
-            query = q_all[k].reshape(total_rows, HD)
-        else:
-            parts = block // own
-            query = q_all[k, pl.ds(at * parts, parts)].reshape(block, HD)
-        top = None
-        for start, size in spans:
-            score = lax.dot_general(
-                query,
-                k_buf[k, start : start + size, :],
-                (((1,), (1,)), ((), ())),
-                preferred_element_type=jnp.float32,
-            )
-            for page in range(size // PAGE):
-                j = start // PAGE + page
-                tile = score[:, page * PAGE : (page + 1) * PAGE] * scale + bias[j : j + 1, :]
-                scores[:, j * PAGE : (j + 1) * PAGE] = tile
-                top = tile if top is None else jnp.maximum(top, tile)
-        score = lax.dot_general(
-            query,
-            k_buf[k, cached:, :],
-            (((1,), (1,)), ((), ())),
-            preferred_element_type=jnp.float32,
-        )
+    keys = cached + PAGE
+    spans = [(start, min(BLOCK, keys - start)) for start in range(0, keys, BLOCK)]
+    parts = block // own
+
+    for k in range(kvh):
+        cache_copy(cache_k_ref, k_buf, k_sem, k).wait()
+        k_turned[k] = k_buf[k].T
+
+    def mask_new(score, at):
         row = at * block + lax.broadcasted_iota(jnp.int32, (block, PAGE), 0)
         column = lax.broadcasted_iota(jnp.int32, (block, PAGE), 1)
         token = (row // own) * rows + row % rows
         allowed = (column < rows) & (me * rows + column <= token)
-        last = jnp.where(allowed, score * scale, FLOOR)
-        top = jnp.max(jnp.maximum(top, last), axis=1, keepdims=True)
-        weight = jnp.exp2(last - top)
-        summed = weight
-        mixed = jnp.dot(
-            weight.astype(jnp.bfloat16), v_buf[k, cached:, :], preferred_element_type=jnp.float32
-        )
+        return jnp.where(allowed, score * scale, FLOOR)
+
+    def step(ahead, now, at):
+        held = pl.ds(at * block, block)
+        if ahead is not None:
+            query = q_all[ahead, pl.ds(at * parts, parts)].reshape(block, HD)
+            slot = lax.rem(ahead, 2)
+            top = None
+        if now is not None:
+            slot_now = lax.rem(now, 2)
+            top_now = tops[slot_now, held, :]
+            summed = jnp.zeros((block, PAGE), jnp.float32)
+            mixed = jnp.zeros((block, HD), jnp.float32)
         for start, size in spans:
-            weight = jnp.exp2(scores[:, start : start + size] - top)
-            for page in range(size // PAGE):
-                summed = summed + weight[:, page * PAGE : (page + 1) * PAGE]
-            mixed = mixed + jnp.dot(
-                weight.astype(jnp.bfloat16),
-                v_buf[k, start : start + size, :],
-                preferred_element_type=jnp.float32,
-            )
-        total = jnp.sum(summed, axis=1, keepdims=True)
-        mixed = mixed * (1.0 / total)
-        lanes = lax.broadcasted_iota(jnp.int32, (2 * own, 128), 1)
-        columns = jnp.zeros((2 * own, 128), jnp.float32)
-        for i in range(block // own):
-            piece = slice(i * own, (i + 1) * own)
-            slot = at * (block // own) + i
-            part[k, slot] = mixed[piece].astype(jnp.bfloat16)
-            column = jnp.concatenate([top[piece], total[piece]], axis=0)
-            columns = jnp.where(lanes == i, column, columns)
-        turned = columns.T
-        for i in range(block // own):
-            stat[k, at * (block // own) + i] = turned[i : i + 1, :]
+            if ahead is not None:
+                score = jnp.dot(
+                    query,
+                    k_turned[ahead, :, start : start + size],
+                    preferred_element_type=jnp.float32,
+                )
+                for page in range(size // PAGE):
+                    j = start // PAGE + page
+                    tile = score[:, page * PAGE : (page + 1) * PAGE]
+                    if j < pages:
+                        tile = tile * scale + bias[j : j + 1, :]
+                    else:
+                        tile = mask_new(tile, at)
+                    scores[slot, held, j * PAGE : (j + 1) * PAGE] = tile
+                    top = tile if top is None else jnp.maximum(top, tile)
+            if now is not None:
+                weights = []
+                for at_key in range(start, start + size, PAGE):
+                    weight = jnp.exp2(scores[slot_now, held, at_key : at_key + PAGE] - top_now)
+                    summed = summed + weight
+                    weights.append(weight.astype(jnp.bfloat16))
+                mixed = mixed + jnp.dot(
+                    jnp.concatenate(weights, axis=1),
+                    v_buf[now, start : start + size, :],
+                    preferred_element_type=jnp.float32,
+                )
+        if ahead is not None:
+            top = jnp.max(top, axis=1, keepdims=True)
+            tops[slot, held, :] = jnp.broadcast_to(top, (block, PAGE))
+        if now is not None:
+            total = jnp.sum(summed, axis=1, keepdims=True)
+            mixed = mixed * (1.0 / total)
+            level = top_now + jnp.log(total) * math.log2(math.e)
+            lanes = lax.broadcasted_iota(jnp.int32, (own, HD), 1)
+            columns = jnp.zeros((own, HD), jnp.float32)
+            for i in range(parts):
+                piece = slice(i * own, (i + 1) * own)
+                part[now, at * parts + i] = mixed[piece].astype(jnp.bfloat16)
+                columns = jnp.where(lanes == i, level[piece], columns)
+            turned = columns.T
+            for i in range(parts):
+                stat[now, at * parts + i] = turned[i : i + 1, :]
+
+    def run(ahead, now):
+        if ahead is not None:
+            for off in range(1, count):
+                q_copy(ahead, off).wait_recv()
+        if now is not None:
+            cache_copy(cache_v_ref, v_buf, v_sem, now).wait()
+        if total_rows == block:
+            step(ahead, now, 0)
+        else:
+            lax.fori_loop(0, total_rows // block, lambda at, c: (step(ahead, now, at), c)[1], 0)
+        if now is not None:
+            for off in range(1, count):
+                part_copy(now, off).start()
+                stat_copy(now, off).start()
+            part_in[now, me] = part[now, me]
+            stat_in[now, me] = stat[now, me]
 
     own_q.wait()
-
-    def one_head(k, carry):
-        for off in range(1, count):
-            q_copy(k, off).wait_recv()
-        cache_copy(cache_k_ref, k_buf, k_sem, k).wait()
-        cache_copy(cache_v_ref, v_buf, v_sem, k).wait()
-        if total_rows == block:
-            attend(k, 0)
-        else:
-            lax.fori_loop(0, total_rows // block, lambda at, c: (attend(k, at), c)[1], 0)
-        for off in range(1, count):
-            part_copy(k, off).start()
-            stat_copy(k, off).start()
-        part_in[k, me] = part[k, me]
-        stat_in[k, me] = stat[k, me]
-        return carry
-
-    lax.fori_loop(0, kvh, one_head, 0)
+    run(0, None)
+    lax.fori_loop(0, kvh - 1, lambda k, c: (run(k + 1, k), c)[1], 0)
+    run(None, kvh - 1)
 
     def combine(k, carry):
         for off in range(1, count):
             part_copy(k, off).wait_recv()
             stat_copy(k, off).wait_recv()
-        tops = [stat_in[k, s] for s in range(count)]
-        totals = [pltpu.roll(t, own, 1) for t in tops]
-        top = functools.reduce(jnp.maximum, tops)
-        shares = [jnp.exp2(t - top) * l for t, l in zip(tops, totals)]
+        levels = [stat_in[k, s] for s in range(count)]
+        top = functools.reduce(jnp.maximum, levels)
+        shares = [jnp.exp2(level - top) for level in levels]
         share = 1.0 / functools.reduce(jnp.add, shares)
         for s in range(count):
             weigh[s : s + 1, :] = shares[s] * share
         turned = weigh[...].T
         result = jnp.zeros((own, HD), jnp.float32)
         for s in range(count):
-            result = result + part_in[k, s].astype(jnp.float32) * turned[0:own, s : s + 1]
+            result = result + part_in[k, s].astype(jnp.float32) * turned[:, s : s + 1]
         out_ref[k] = result.astype(out_ref.dtype)
         return carry
 
     weigh[...] = jnp.zeros_like(weigh)
-    lax.fori_loop(0, kvh, combine, 0)
-
+    lax.fori_loop(0, kvh - 1, combine, 0)
     for k in range(kvh):
         for off in range(1, count):
             q_copy(k, off).wait_send()
             part_copy(k, off).wait_send()
             stat_copy(k, off).wait_send()
+    combine(kvh - 1, 0)
 
 
 def local(queries, new_keys, new_values, cache_keys, cache_values, cache_length, page_table):
@@ -279,14 +292,16 @@
             pltpu.VMEM((PAGE, HD), jnp.float32),
             pltpu.VMEM((kvh, count, own, HD), jnp.bfloat16),
             pltpu.VMEM((kvh, cached + PAGE, HD), jnp.bfloat16),
+            pltpu.VMEM((kvh, HD, cached + PAGE), jnp.bfloat16),
             pltpu.VMEM((kvh, cached + PAGE, HD), jnp.bfloat16),
             pltpu.VMEM((pages, PAGE), jnp.float32),
-            pltpu.VMEM((block, cached), jnp.float32),
+            pltpu.VMEM((2, count * own, cached + PAGE), jnp.float32),
+            pltpu.VMEM((2, count * own, PAGE), jnp.float32),
             pltpu.VMEM((kvh, count, own, HD), jnp.bfloat16),
-            pltpu.VMEM((kvh, count, 1, 2 * own), jnp.float32),
+            pltpu.VMEM((kvh, count, 1, own), jnp.float32),
             pltpu.VMEM((kvh, count, own, HD), jnp.bfloat16),
-            pltpu.VMEM((kvh, count, 1, 2 * own), jnp.float32),
-            pltpu.VMEM((128, 2 * own), jnp.float32),
+            pltpu.VMEM((kvh, count, 1, own), jnp.float32),
+            pltpu.VMEM((HD, own), jnp.float32),
             dma((5,)),
             dma((kvh,)),
             dma((kvh,)),

time: 21.9 us -> 24 us (1.096)
  Pallas kernels: 20.4 us -> 22.6 us
    pallas_call x1, Pallas kernels: 20.4 us -> 22.6 us  [local(): pl.pallas_call(functools.partial(kernel, count), out_shape=pltpu.VMEM((kv...]
where the time goes in v5:
time: 24 us; the launch traced here: 23.9 us
  Pallas kernels  22.6 us (94%)
  between operations  0.66 us (3%)
  local copies, waits for them, and re-layouts  0.63 us (3%)
    pallas_call x1, Pallas kernels, local(): pl.pallas_call(functools.partial(kernel, count), out_shape=pltpu.VMEM((kv...  22.6 us
    unnamed x1, local copies, waits for them, and re-layouts  0.63 us

profile of v5, /device:TPU:0, one launch (start us, length us, event | category | flops | bytes accessed | tf_op | source)
XLA Modules:
  0.0 23.9 jit_solution(528943160394616094)
XLA Ops:
  0.7 22.6 %paged_attention.1 = bf16[4,64,128]{2,1,0:T(8,128)(2,1)S(1)} custom-call(bf16[4,64,128]{2,1,0:T(8,128)(2,1)} %bitcast.18, bf16[4,4,128]{2,1,0:T(4,128)(2,1)} %bitcast.19, bf16[4,4,128]{2,1,0:T(4,128)(2,1)} %bitcast.20, bf16[2048,512]{1,0:T(8,128)(2,1)} %cache_k_ref.1, bf16[2048,512]{1,0:T(8,128)(2,1)} %cache_v_ref.1, s32[1]{0:T(128)S(6)} %copy.12.length_ref, ...), custom_call_target="tpu_custom_call" | custom-call | flops 1073741824 | bytes 4194304 | tf_op jit(solution)/shard_map/paged_attention/pallas_call | solution.py:282
  23.2 0.6 %copy.11 = bf16[4,8192]{1,0:T(4,128)(2,1)} copy(bf16[4,8192]{1,0:T(4,128)(2,1)S(1)} %bitcast.17) | data formatting | bytes 131072

commit v6 on v2

--- a/solution.py
+++ b/solution.py
@@ -86,9 +86,8 @@
     for copy in small:
         copy.start()
     own_q.start()
-    for k in range(kvh):
-        cache_copy(cache_k_ref, k_buf, k_sem, k).start()
-        cache_copy(cache_v_ref, v_buf, v_sem, k).start()
+    cache_copy(cache_k_ref, k_buf, k_sem, 0).start()
+    cache_copy(cache_v_ref, v_buf, v_sem, 0).start()
     pl.semaphore_wait(barrier, count - 1)
 
     def q_copy(k, off):
@@ -126,6 +125,9 @@
     for k in range(kvh):
         for off in range(1, count):
             q_copy(k, off).start()
+    for k in range(1, kvh):
+        cache_copy(cache_k_ref, k_buf, k_sem, k).start()
+        cache_copy(cache_v_ref, v_buf, v_sem, k).start()
 
     for copy in small:
         copy.wait()
@@ -193,14 +195,13 @@
             )
         total = jnp.sum(summed, axis=1, keepdims=True)
         mixed = mixed * (1.0 / total)
-        lanes = lax.broadcasted_iota(jnp.int32, (2 * own, 128), 1)
-        columns = jnp.zeros((2 * own, 128), jnp.float32)
+        level = top + jnp.log(total) * math.log2(math.e)
+        lanes = lax.broadcasted_iota(jnp.int32, (own, HD), 1)
+        columns = jnp.zeros((own, HD), jnp.float32)
         for i in range(block // own):
             piece = slice(i * own, (i + 1) * own)
-            slot = at * (block // own) + i
-            part[k, slot] = mixed[piece].astype(jnp.bfloat16)
-            column = jnp.concatenate([top[piece], total[piece]], axis=0)
-            columns = jnp.where(lanes == i, column, columns)
+            part[k, at * (block // own) + i] = mixed[piece].astype(jnp.bfloat16)
+            columns = jnp.where(lanes == i, level[piece], columns)
         turned = columns.T
         for i in range(block // own):
             stat[k, at * (block // own) + i] = turned[i : i + 1, :]
@@ -229,28 +230,27 @@
         for off in range(1, count):
             part_copy(k, off).wait_recv()
             stat_copy(k, off).wait_recv()
-        tops = [stat_in[k, s] for s in range(count)]
-        totals = [pltpu.roll(t, own, 1) for t in tops]
-        top = functools.reduce(jnp.maximum, tops)
-        shares = [jnp.exp2(t - top) * l for t, l in zip(tops, totals)]
+        levels = [stat_in[k, s] for s in range(count)]
+        top = functools.reduce(jnp.maximum, levels)
+        shares = [jnp.exp2(level - top) for level in levels]
         share = 1.0 / functools.reduce(jnp.add, shares)
         for s in range(count):
             weigh[s : s + 1, :] = shares[s] * share
         turned = weigh[...].T
         result = jnp.zeros((own, HD), jnp.float32)
         for s in range(count):
-            result = result + part_in[k, s].astype(jnp.float32) * turned[0:own, s : s + 1]
+            result = result + part_in[k, s].astype(jnp.float32) * turned[:, s : s + 1]
         out_ref[k] = result.astype(out_ref.dtype)
         return carry
 
     weigh[...] = jnp.zeros_like(weigh)
-    lax.fori_loop(0, kvh, combine, 0)
-
+    lax.fori_loop(0, kvh - 1, combine, 0)
     for k in range(kvh):
         for off in range(1, count):
             q_copy(k, off).wait_send()
             part_copy(k, off).wait_send()
             stat_copy(k, off).wait_send()
+    combine(kvh - 1, 0)
 
 
 def local(queries, new_keys, new_values, cache_keys, cache_values, cache_length, page_table):
@@ -283,10 +283,10 @@
             pltpu.VMEM((pages, PAGE), jnp.float32),
             pltpu.VMEM((block, cached), jnp.float32),
             pltpu.VMEM((kvh, count, own, HD), jnp.bfloat16),
-            pltpu.VMEM((kvh, count, 1, 2 * own), jnp.float32),
+            pltpu.VMEM((kvh, count, 1, own), jnp.float32),
             pltpu.VMEM((kvh, count, own, HD), jnp.bfloat16),
-            pltpu.VMEM((kvh, count, 1, 2 * own), jnp.float32),
-            pltpu.VMEM((128, 2 * own), jnp.float32),
+            pltpu.VMEM((kvh, count, 1, own), jnp.float32),
+            pltpu.VMEM((HD, own), jnp.float32),
             dma((5,)),
             dma((kvh,)),
             dma((kvh,)),

time: 21.9 us -> 21.8 us (level)
  no operation moved by 1% of the time
where the time goes in v6:
time: 21.8 us; the launch traced here: 21.7 us
  Pallas kernels  20.4 us (94%)
  between operations  0.66 us (3%)
  local copies, waits for them, and re-layouts  0.63 us (3%)
    pallas_call x1, Pallas kernels, local(): pl.pallas_call(functools.partial(kernel, count), out_shape=pltpu.VMEM((kv...  20.4 us
    unnamed x1, local copies, waits for them, and re-layouts  0.63 us

profile of v6, /device:TPU:0, one launch (start us, length us, event | category | flops | bytes accessed | tf_op | source)
XLA Modules:
  0.0 21.7 jit_solution(11141042945052138403)
XLA Ops:
  0.7 20.4 %paged_attention.1 = bf16[4,64,128]{2,1,0:T(8,128)(2,1)S(1)} custom-call(bf16[4,64,128]{2,1,0:T(8,128)(2,1)} %bitcast.18, bf16[4,4,128]{2,1,0:T(4,128)(2,1)} %bitcast.19, bf16[4,4,128]{2,1,0:T(4,128)(2,1)} %bitcast.20, bf16[2048,512]{1,0:T(8,128)(2,1)} %cache_k_ref.1, bf16[2048,512]{1,0:T(8,128)(2,1)} %cache_v_ref.1, s32[1]{0:T(128)S(6)} %copy.12.length_ref, ...), custom_call_target="tpu_custom_call" | custom-call | flops 1073741824 | bytes 4194304 | tf_op jit(solution)/shard_map/paged_attention/pallas_call | solution.py:269
  21.0 0.6 %copy.11 = bf16[4,8192]{1,0:T(4,128)(2,1)} copy(bf16[4,8192]{1,0:T(4,128)(2,1)S(1)} %bitcast.17) | data formatting | bytes 131072

commit v7 on v6

--- a/solution.py
+++ b/solution.py
@@ -12,6 +12,7 @@
 PAGE = 128
 FLOOR = -1e30
 BLOCK = 256
+ROWS = 128
 
 
 def kernel(
@@ -33,6 +34,7 @@
     k_buf,
     v_buf,
     bias,
+    bias_new,
     scores,
     part,
     stat,
@@ -55,12 +57,15 @@
     cached = cache_k_ref.shape[0]
     pages = cached // PAGE
     total_rows = count * own
-    block = min(BLOCK, total_rows)
+    block = min(ROWS, total_rows)
     scale = HD ** (-0.5) * math.log2(math.e)
+
+    def each_head(body):
+        lax.fori_loop(0, kvh, lambda k, carry: (body(k), carry)[1], 0)
 
     def cache_copy(source, target, sems, k):
         return pltpu.make_async_copy(
-            source.at[:, pl.ds(k * HD, HD)], target.at[k, pl.ds(0, cached)], sems.at[k]
+            source.at[:, pl.ds(pl.multiple_of(k * HD, HD), HD)], target.at[k, pl.ds(0, cached)], sems.at[k]
         )
 
     barrier = pltpu.get_barrier_semaphore()
@@ -122,17 +127,23 @@
             device_id_type=pl.DeviceIdType.MESH,
         )
 
-    for k in range(kvh):
+    @each_head
+    def _(k):
         for off in range(1, count):
             q_copy(k, off).start()
-    for k in range(1, kvh):
+
+    @functools.partial(lax.fori_loop, 1, kvh, init_val=0)
+    def _(k, carry):
         cache_copy(cache_k_ref, k_buf, k_sem, k).start()
         cache_copy(cache_v_ref, v_buf, v_sem, k).start()
+        return carry
+
 
     for copy in small:
         copy.wait()
     tail[...] = jnp.zeros_like(tail)
-    for k in range(kvh):
+    @each_head
+    def _(k):
         tail[0:rows, :] = new_k[k].astype(jnp.float32)
         k_buf[k, cached:, :] = tail[...].astype(jnp.bfloat16)
         tail[0:rows, :] = new_v[k].astype(jnp.float32)
@@ -145,6 +156,12 @@
     logical = jnp.sum(hits, axis=1, keepdims=True)
     lane = lax.broadcasted_iota(jnp.int32, (pages, PAGE), 1)
     bias[...] = jnp.where(logical * PAGE + lane < length, 0.0, FLOOR)
+
+    token = lax.rem(lax.broadcasted_iota(jnp.int32, (own, PAGE), 0), rows)
+    column = lax.broadcasted_iota(jnp.int32, (own, PAGE), 1)
+    first = jnp.where(column < rows, me * rows + column - token, count * rows)
+    for s in range(count):
+        bias_new[s] = jnp.where(first <= s * rows, 0.0, FLOOR)
 
     spans = [(at, min(BLOCK, cached - at)) for at in range(0, cached, BLOCK)]
 
@@ -173,11 +190,8 @@
             (((1,), (1,)), ((), ())),
             preferred_element_type=jnp.float32,
         )
-        row = at * block + lax.broadcasted_iota(jnp.int32, (block, PAGE), 0)
-        column = lax.broadcasted_iota(jnp.int32, (block, PAGE), 1)
-        token = (row // own) * rows + row % rows
-        allowed = (column < rows) & (me * rows + column <= token)
-        last = jnp.where(allowed, score * scale, FLOOR)
+        barred = bias_new[pl.ds(at * (block // own), block // own)].reshape(block, PAGE)
+        last = score * scale + barred
         top = jnp.max(jnp.maximum(top, last), axis=1, keepdims=True)
         weight = jnp.exp2(last - top)
         summed = weight
@@ -230,6 +244,10 @@
         for off in range(1, count):
             part_copy(k, off).wait_recv()
             stat_copy(k, off).wait_recv()
+        for off in range(1, count):
+            q_copy(k, off).wait_send()
+            part_copy(k, off).wait_send()
+            stat_copy(k, off).wait_send()
         levels = [stat_in[k, s] for s in range(count)]
         top = functools.reduce(jnp.maximum, levels)
         shares = [jnp.exp2(level - top) for level in levels]
@@ -244,13 +262,7 @@
         return carry
 
     weigh[...] = jnp.zeros_like(weigh)
-    lax.fori_loop(0, kvh - 1, combine, 0)
-    for k in range(kvh):
-        for off in range(1, count):
-            q_copy(k, off).wait_send()
-            part_copy(k, off).wait_send()
-            stat_copy(k, off).wait_send()
-    combine(kvh - 1, 0)
+    lax.fori_loop(0, kvh, combine, 0)
 
 
 def local(queries, new_keys, new_values, cache_keys, cache_values, cache_length, page_table):
@@ -261,7 +273,7 @@
     kvh = cache_keys.shape[1] // HD
     group = heads // kvh
     own = rows * group
-    block = min(BLOCK, count * own)
+    block = min(ROWS, count * own)
     pages = cached // PAGE
     vmem = pl.BlockSpec(memory_space=pltpu.VMEM)
     held = pl.BlockSpec(memory_space=pltpu.HBM)
@@ -281,6 +293,7 @@
             pltpu.VMEM((kvh, cached + PAGE, HD), jnp.bfloat16),
             pltpu.VMEM((kvh, cached + PAGE, HD), jnp.bfloat16),
             pltpu.VMEM((pages, PAGE), jnp.float32),
+            pltpu.VMEM((count, own, PAGE), jnp.float32),
             pltpu.VMEM((block, cached), jnp.float32),
             pltpu.VMEM((kvh, count, own, HD), jnp.bfloat16),
             pltpu.VMEM((kvh, count, 1, own), jnp.float32),

time: 21.8 us -> 22.9 us (1.050)
  Pallas kernels: 20.4 us -> 21.4 us
    pallas_call x1, Pallas kernels: 20.4 us -> 21.4 us  [local(): pl.pallas_call(functools.partial(kernel, count), out_shape=pltpu.VMEM((kv...]
where the time goes in v7:
time: 22.9 us; the launch traced here: 22.7 us
  Pallas kernels  21.4 us (93%)
  between operations  0.66 us (3%)
  local copies, waits for them, and re-layouts  0.63 us (3%)
    pallas_call x1, Pallas kernels, local(): pl.pallas_call(functools.partial(kernel, count), out_shape=pltpu.VMEM((kv...  21.4 us
    unnamed x1, local copies, waits for them, and re-layouts  0.63 us

profile of v7, /device:TPU:0, one launch (start us, length us, event | category | flops | bytes accessed | tf_op | source)
XLA Modules:
  0.0 22.7 jit_solution(9630352559474720585)
XLA Ops:
  0.7 21.4 %paged_attention.1 = bf16[4,64,128]{2,1,0:T(8,128)(2,1)S(1)} custom-call(bf16[4,64,128]{2,1,0:T(8,128)(2,1)} %bitcast.18, bf16[4,4,128]{2,1,0:T(4,128)(2,1)} %bitcast.19, bf16[4,4,128]{2,1,0:T(4,128)(2,1)} %bitcast.20, bf16[2048,512]{1,0:T(8,128)(2,1)} %cache_k_ref.1, bf16[2048,512]{1,0:T(8,128)(2,1)} %cache_v_ref.1, s32[1]{0:T(128)S(6)} %copy.12.length_ref, ...), custom_call_target="tpu_custom_call" | custom-call | flops 1073741824 | bytes 4194304 | tf_op jit(solution)/shard_map/paged_attention/pallas_call | solution.py:281
  22.1 0.6 %copy.11 = bf16[4,8192]{1,0:T(4,128)(2,1)} copy(bf16[4,8192]{1,0:T(4,128)(2,1)S(1)} %bitcast.17) | data formatting | bytes 131072

commit v8 on v7

--- a/solution.py
+++ b/solution.py
@@ -12,7 +12,7 @@
 PAGE = 128
 FLOOR = -1e30
 BLOCK = 256
-ROWS = 128
+ROWS = 256
 
 
 def kernel(

time: 22.9 us -> 21.9 us (0.956)
  Pallas kernels: 21.4 us -> 20.4 us
    pallas_call x1, Pallas kernels: 21.4 us -> 20.4 us  [local(): pl.pallas_call(functools.partial(kernel, count), out_shape=pltpu.VMEM((kv...]
where the time goes in v8:
time: 21.9 us; the launch traced here: 21.7 us
  Pallas kernels  20.4 us (93%)
  between operations  0.66 us (3%)
  local copies, waits for them, and re-layouts  0.63 us (3%)
    pallas_call x1, Pallas kernels, local(): pl.pallas_call(functools.partial(kernel, count), out_shape=pltpu.VMEM((kv...  20.4 us
    unnamed x1, local copies, waits for them, and re-layouts  0.63 us

profile of v8, /device:TPU:0, one launch (start us, length us, event | category | flops | bytes accessed | tf_op | source)
XLA Modules:
  0.0 21.7 jit_solution(16564744041634363565)
XLA Ops:
  0.7 20.4 %paged_attention.1 = bf16[4,64,128]{2,1,0:T(8,128)(2,1)S(1)} custom-call(bf16[4,64,128]{2,1,0:T(8,128)(2,1)} %bitcast.18, bf16[4,4,128]{2,1,0:T(4,128)(2,1)} %bitcast.19, bf16[4,4,128]{2,1,0:T(4,128)(2,1)} %bitcast.20, bf16[2048,512]{1,0:T(8,128)(2,1)} %cache_k_ref.1, bf16[2048,512]{1,0:T(8,128)(2,1)} %cache_v_ref.1, s32[1]{0:T(128)S(6)} %copy.12.length_ref, ...), custom_call_target="tpu_custom_call" | custom-call | flops 1073741824 | bytes 4194304 | tf_op jit(solution)/shard_map/paged_attention/pallas_call | solution.py:281
  21.1 0.6 %copy.11 = bf16[4,8192]{1,0:T(4,128)(2,1)} copy(bf16[4,8192]{1,0:T(4,128)(2,1)S(1)} %bitcast.17) | data formatting | bytes 131072

commit v9 on v8

--- a/solution.py
+++ b/solution.py
@@ -36,6 +36,7 @@
     bias,
     bias_new,
     scores,
+    weights,
     part,
     stat,
     part_in,
@@ -194,19 +195,14 @@
         last = score * scale + barred
         top = jnp.max(jnp.maximum(top, last), axis=1, keepdims=True)
         weight = jnp.exp2(last - top)
+        weights[:, cached:] = weight.astype(jnp.bfloat16)
         summed = weight
-        mixed = jnp.dot(
-            weight.astype(jnp.bfloat16), v_buf[k, cached:, :], preferred_element_type=jnp.float32
-        )
         for start, size in spans:
             weight = jnp.exp2(scores[:, start : start + size] - top)
             for page in range(size // PAGE):
                 summed = summed + weight[:, page * PAGE : (page + 1) * PAGE]
-            mixed = mixed + jnp.dot(
-                weight.astype(jnp.bfloat16),
-                v_buf[k, start : start + size, :],
-                preferred_element_type=jnp.float32,
-            )
+            weights[:, start : start + size] = weight.astype(jnp.bfloat16)
+        mixed = jnp.dot(weights[...], v_buf[k], preferred_element_type=jnp.float32)
         total = jnp.sum(summed, axis=1, keepdims=True)
         mixed = mixed * (1.0 / total)
         level = top + jnp.log(total) * math.log2(math.e)
@@ -295,6 +291,7 @@
             pltpu.VMEM((pages, PAGE), jnp.float32),
             pltpu.VMEM((count, own, PAGE), jnp.float32),
             pltpu.VMEM((block, cached), jnp.float32),
+            pltpu.VMEM((block, cached + PAGE), jnp.bfloat16),
             pltpu.VMEM((kvh, count, own, HD), jnp.bfloat16),
             pltpu.VMEM((kvh, count, 1, own), jnp.float32),
             pltpu.VMEM((kvh, count, own, HD), jnp.bfloat16),

time: 21.9 us -> 22.1 us (level)
  no operation moved by 1% of the time
where the time goes in v9:
time: 22.1 us; the launch traced here: 21.9 us
  Pallas kernels  20.6 us (93%)
  between operations  0.66 us (3%)
  local copies, waits for them, and re-layouts  0.63 us (3%)
    pallas_call x1, Pallas kernels, local(): pl.pallas_call(functools.partial(kernel, count), out_shape=pltpu.VMEM((kv...  20.6 us
    unnamed x1, local copies, waits for them, and re-layouts  0.63 us

profile of v9, /device:TPU:0, one launch (start us, length us, event | category | flops | bytes accessed | tf_op | source)
XLA Modules:
  0.0 21.9 jit_solution(12040470150626909243)
XLA Ops:
  0.7 20.6 %paged_attention.1 = bf16[4,64,128]{2,1,0:T(8,128)(2,1)S(1)} custom-call(bf16[4,64,128]{2,1,0:T(8,128)(2,1)} %bitcast.18, bf16[4,4,128]{2,1,0:T(4,128)(2,1)} %bitcast.19, bf16[4,4,128]{2,1,0:T(4,128)(2,1)} %bitcast.20, bf16[2048,512]{1,0:T(8,128)(2,1)} %cache_k_ref.1, bf16[2048,512]{1,0:T(8,128)(2,1)} %cache_v_ref.1, s32[1]{0:T(128)S(6)} %copy.12.length_ref, ...), custom_call_target="tpu_custom_call" | custom-call | flops 1073741824 | bytes 4194304 | tf_op jit(solution)/shard_map/paged_attention/pallas_call | solution.py:277
  21.3 0.6 %copy.11 = bf16[4,8192]{1,0:T(4,128)(2,1)} copy(bf16[4,8192]{1,0:T(4,128)(2,1)S(1)} %bitcast.17) | data formatting | bytes 131072

commit v10 on v3

--- a/solution.py
+++ b/solution.py
@@ -44,6 +44,8 @@
     v_sem,
     q_send,
     q_recv,
+    far_send,
+    far_recv,
     cross_send,
     cross_recv,
     pass_send,
@@ -115,6 +117,16 @@
             device_id_type=pl.DeviceIdType.MESH,
         )
 
+    def far_copy(target, slot):
+        return pltpu.make_async_remote_copy(
+            src_ref=q_ref.at[0],
+            dst_ref=q_all.at[0, me],
+            send_sem=far_send.at[target],
+            recv_sem=far_recv.at[slot],
+            device_id={"ctx": other + target},
+            device_id_type=pl.DeviceIdType.MESH,
+        )
+
     def cross_copy(k, slot):
         return pltpu.make_async_remote_copy(
             src_ref=q_ref.at[k],
@@ -164,7 +176,10 @@
         )
 
     for k in range(kvh):
-        if halves == 2:
+        if halves == 2 and k == 0:
+            for target in range(half):
+                far_copy(target, me - base).start()
+        elif halves == 2:
             cross_copy(k, me - base).start()
         for off in range(1, half):
             q_copy(k, off).start()
@@ -250,8 +265,6 @@
             stat[k, at * (block // own) + i] = turned[i : i + 1, :]
 
     own_q.wait()
-    if halves == 2:
-        pl.when(relay)(lambda: pass_on(0))
 
     def pass_next(k):
         if halves == 2:
@@ -260,9 +273,16 @@
     def one_head(k, carry):
         for off in range(1, half):
             q_copy(k, off).wait_recv()
+        if halves == 2:
+
+            @pl.when(k == 0)
+            def _():
+                for slot in range(half):
+                    far_copy(0, slot).wait_recv()
+
         if halves == 2 and half > 1:
 
-            @pl.when(jnp.logical_not(relay))
+            @pl.when(jnp.logical_not(relay) & (k > 0))
             def _():
                 pass_copy(k, 1).wait_recv()
 
@@ -310,12 +330,14 @@
             part_copy(k, off).wait_send()
             stat_copy(k, off).wait_send()
     if halves == 2:
-        for k in range(kvh):
+        for target in range(half):
+            far_copy(target, 0).wait_send()
+        for k in range(1, kvh):
             cross_copy(k, 0).wait_send()
 
         @pl.when(relay)
         def _():
-            for k in range(kvh):
+            for k in range(1, kvh):
                 for off in range(1, half):
                     pass_copy(k, off).wait_send()
 
@@ -360,6 +382,8 @@
             dma((kvh,)),
             dma((kvh, max(half - 1, 1))),
             dma((kvh, max(half - 1, 1))),
+            dma((half,)),
+            dma((half,)),
             dma((kvh,)),
             dma((kvh, half)),
             dma((kvh, max(half - 1, 1))),

time: 23.2 us -> 23.1 us (level)
  no operation moved by 1% of the time
where the time goes in v10:
time: 23.1 us; the launch traced here: 22.9 us
  Pallas kernels  21.6 us (94%)
  between operations  0.66 us (3%)
  local copies, waits for them, and re-layouts  0.63 us (3%)
    pallas_call x1, Pallas kernels, local(): pl.pallas_call(functools.partial(kernel, count), out_shape=pltpu.VMEM((kv...  21.6 us
    unnamed x1, local copies, waits for them, and re-layouts  0.63 us

profile of v10, /device:TPU:0, one launch (start us, length us, event | category | flops | bytes accessed | tf_op | source)
XLA Modules:
  0.0 22.9 jit_solution(15549328515643527864)
XLA Ops:
  0.7 21.6 %paged_attention.1 = bf16[4,64,128]{2,1,0:T(8,128)(2,1)S(1)} custom-call(bf16[4,64,128]{2,1,0:T(8,128)(2,1)} %bitcast.18, bf16[4,4,128]{2,1,0:T(4,128)(2,1)} %bitcast.19, bf16[4,4,128]{2,1,0:T(4,128)(2,1)} %bitcast.20, bf16[2048,512]{1,0:T(8,128)(2,1)} %cache_k_ref.1, bf16[2048,512]{1,0:T(8,128)(2,1)} %cache_v_ref.1, s32[1]{0:T(128)S(6)} %copy.12.length_ref, ...), custom_call_target="tpu_custom_call" | custom-call | flops 1073741824 | bytes 4194304 | tf_op jit(solution)/shard_map/paged_attention/pallas_call | solution.py:359
  22.3 0.6 %copy.11 = bf16[4,8192]{1,0:T(4,128)(2,1)} copy(bf16[4,8192]{1,0:T(4,128)(2,1)S(1)} %bitcast.17) | data formatting | bytes 131072
